TPU v7x, 256 devices: a whole 4x4x8 slice. The times are simulated.
256 devices in a mesh: clip: 2 (over y_lo), patch: 16 (over z, core), frame: 8 (over y_hi, x).
Axes of the slice: x: 4, y: 4 (y_hi: 2, y_lo: 2; y = y_hi * 2 + y_lo), z: 8, core: 2. Of those that a mesh axis runs over, the one named last changes fastest.
Arguments:
- queries: bfloat16 [4, 16, 1024, 2048], P('clip', 'frame', 'patch'), may hold values from -48 to 48, as said below
- keys: bfloat16 [4, 16, 1024, 2048], P('clip', 'frame', 'patch'), may hold values from -48 to 48, as said below
- values: bfloat16 [4, 16, 1024, 2048], P('clip', 'frame', 'patch'), may hold values from -6 to 6
- grad_out: bfloat16 [4, 16, 1024, 2048], P('clip', 'frame', 'patch'), may hold values from -6 to 6
- gain_q: float32 [16, 128], P('patch'), may hold values from 0.5 to 5.5, as said below
- gain_k: float32 [16, 128], P('patch'), may hold values from 0.5 to 5.5, as said below
Outputs:
- grad_queries: bfloat16 [4, 16, 1024, 2048], P('clip', 'frame', 'patch')
- grad_keys: bfloat16 [4, 16, 1024, 2048], P('clip', 'frame', 'patch')
- grad_values: bfloat16 [4, 16, 1024, 2048], P('clip', 'frame', 'patch')
- gain_grads: float32 [2, 16, 128], P(None, 'patch')
Inputs may be any that keep to these rules, and one draw needn't show every extreme that they name: `queries`: finite real values. `keys`: finite real values. `gain_q`: positive gains. `gain_k`: positive gains.
All inputs are finite; a program needn't handle non-finite values.
Results may differ from a plain program's by a relative error of at most 0.034.
The roundings to bfloat16 on the way count: a program that leaves them out, or rounds other values in their place, can miss the bound.
Values may be sent and summed in bfloat16 or wider, within the bound.
No kernel may reach another device: no remote copies, remote signals or barrier semaphores. Data moves between devices by JAX's collectives and lax.ppermute only.
A program may use at most 128 MiB of HBM per device.

v0:
```python
import math

import jax
import jax.numpy as jnp
from jax import lax
from jax.sharding import PartitionSpec as P

EPS = 1e-06


def normalize(raw, gain):
    wide = raw.astype(jnp.float32)
    scale = lax.rsqrt(jnp.mean(wide * wide, axis=-1, keepdims=True) + EPS)
    unit = wide * scale
    return (unit, scale, (unit * gain).astype(jnp.bfloat16))


def restore(grad_norm, unit, scale, gain):
    grad_unit = grad_norm * gain
    along = jnp.mean(grad_unit * unit, axis=-1, keepdims=True)
    return ((scale * (grad_unit - unit * along)).astype(jnp.bfloat16), grad_norm * unit)


def frame_grads(items, gain_q, gain_k):
    queries, keys, values, grad_out = items
    inverse = 1.0 / math.sqrt(queries.shape[-1])
    q_unit, q_scale, q_norm = normalize(queries, gain_q)
    k_unit, k_scale, k_norm = normalize(keys, gain_k)
    scores = (
        jnp.einsum("fpe,fke->fpk", q_norm, k_norm, preferred_element_type=jnp.float32) * inverse
    )
    top = jnp.max(scores, axis=-1, keepdims=True)
    expo = jnp.exp(scores - top)
    prob = expo / jnp.sum(expo, axis=-1, keepdims=True)
    prob_low = prob.astype(jnp.bfloat16)
    dprob = jnp.einsum("fpe,fke->fpk", grad_out, values, preferred_element_type=jnp.float32)
    delta = jnp.sum(prob * dprob, axis=-1, keepdims=True)
    dscore = (prob * (dprob - delta)).astype(jnp.bfloat16)
    grad_v = jnp.einsum(
        "fpk,fpe->fke", prob_low, grad_out, preferred_element_type=jnp.float32
    ).astype(jnp.bfloat16)
    grad_qn = (
        jnp.einsum("fpk,fke->fpe", dscore, k_norm, preferred_element_type=jnp.float32) * inverse
    )
    grad_kn = (
        jnp.einsum("fpk,fpe->fke", dscore, q_norm, preferred_element_type=jnp.float32) * inverse
    )
    grad_q, term_q = restore(grad_qn, q_unit, q_scale, gain_q)
    grad_k, term_k = restore(grad_kn, k_unit, k_scale, gain_k)
    return (grad_q, grad_k, grad_v, jnp.sum(term_q, axis=1), jnp.sum(term_k, axis=1))


def body(queries, keys, values, grad_out, gain_q, gain_k):
    clips, frames, rows, width = queries.shape
    heads = lax.axis_size("patch")
    depth = width // heads
    total = rows * heads
    count = clips * frames
    shaped = tuple(
        (a.reshape(count, rows, heads, depth) for a in (queries, keys, values, grad_out))
    )
    arrived = (
        lax.all_to_all(shaped[0], "patch", split_axis=2, concat_axis=1, tiled=True),
        lax.all_to_all(shaped[1], "patch", split_axis=2, concat_axis=1, tiled=True),
        lax.all_to_all(shaped[2], "patch", split_axis=2, concat_axis=1, tiled=True),
        lax.all_to_all(shaped[3], "patch", split_axis=2, concat_axis=1, tiled=True),
    )
    local = tuple((a.reshape(count, 1, total, depth) for a in arrived))
    grad_q, grad_k, grad_v, term_q, term_k = lax.map(
        lambda items: frame_grads(items, gain_q, gain_k), local
    )
    leaving = tuple((a.reshape(count, total, 1, depth) for a in (grad_q, grad_k, grad_v)))
    out_q, out_k, out_v = (
        lax.all_to_all(leaving[0], "patch", split_axis=1, concat_axis=2, tiled=True),
        lax.all_to_all(leaving[1], "patch", split_axis=1, concat_axis=2, tiled=True),
        lax.all_to_all(leaving[2], "patch", split_axis=1, concat_axis=2, tiled=True),
    )
    partial_value = jnp.stack(
        [jnp.sum(term_q.reshape(-1, depth), axis=0), jnp.sum(term_k.reshape(-1, depth), axis=0)]
    )
    summed = lax.psum(partial_value, ("clip", "frame"))
    gain_grads = summed.reshape(2, 1, depth)
    full = (clips, frames, rows, width)
    return (out_q.reshape(full), out_k.reshape(full), out_v.reshape(full), gain_grads)


def solution(mesh):
    in_specs = (
        P("clip", "frame", "patch", None),
        P("clip", "frame", "patch", None),
        P("clip", "frame", "patch", None),
        P("clip", "frame", "patch", None),
        P("patch", None),
        P("patch", None),
    )
    out_specs = (
        P("clip", "frame", "patch", None),
        P("clip", "frame", "patch", None),
        P("clip", "frame", "patch", None),
        P(None, "patch", None),
    )
    return jax.shard_map(body, mesh=mesh, in_specs=in_specs, out_specs=out_specs, check_vma=False)
```

profile of v0, /device:TPU:32, one launch (start us, length us, event | category | flops | bytes accessed | tf_op | source)
XLA Modules:
  0.0 299.7 jit_solution(4749145237980516503)
XLA Ops:
  0.6 1.5 copy.44
  2.2 1.2 copy.25
  3.4 8.6 %all-to-all-start = ((bf16[4,64,16,128]{3,1,0,2:T(8,128)(2,1)}), bf16[4,64,16,128]{3,1,0,2:T(8,128)(2,1)S(1)}, u32[]{:S(2)}, u32[]{:S(2)}) async-start(bf16[4,64,16,128]{3,1,0,2:T(8,128)(2,1)} %copy.25), calls=%async_computation | async-start | bytes 2097152 | tf_op jit(solution)/shard_map/all_to_all | solution.py:63
  12.3 1.2 copy.27
  13.5 23.3 %all-to-all-done = bf16[4,64,16,128]{3,1,0,2:T(8,128)(2,1)S(1)} async-done(((bf16[4,64,16,128]{3,1,0,2:T(8,128)(2,1)}), bf16[4,64,16,128]{3,1,0,2:T(8,128)(2,1)S(1)}, u32[]{:S(2)}, u32[]{:S(2)}) %all-to-all-start) | async-done | bytes 1048608 | tf_op jit(solution)/shard_map/all_to_all | solution.py:63
  36.8 6.7 %all-to-all-start.1 = ((bf16[4,64,16,128]{3,1,0,2:T(8,128)(2,1)}), bf16[4,64,16,128]{3,1,0,2:T(8,128)(2,1)S(1)}, u32[]{:S(2)}, u32[]{:S(2)}) async-start(bf16[4,64,16,128]{3,1,0,2:T(8,128)(2,1)} %copy.27), calls=%async_computation.1 | async-start | bytes 2097152 | tf_op jit(solution)/shard_map/all_to_all | solution.py:64
  43.5 1.4 copy.46
  44.9 1.2 copy.29
  46.2 22.0 %all-to-all-done.1 = bf16[4,64,16,128]{3,1,0,2:T(8,128)(2,1)S(1)} async-done(((bf16[4,64,16,128]{3,1,0,2:T(8,128)(2,1)}), bf16[4,64,16,128]{3,1,0,2:T(8,128)(2,1)S(1)}, u32[]{:S(2)}, u32[]{:S(2)}) %all-to-all-start.1) | async-done | bytes 1048608 | tf_op jit(solution)/shard_map/all_to_all | solution.py:64
  68.2 6.7 %all-to-all-start.2 = ((bf16[4,64,16,128]{3,1,0,2:T(8,128)(2,1)}), bf16[4,64,16,128]{3,1,0,2:T(8,128)(2,1)S(1)}, u32[]{:S(2)}, u32[]{:S(2)}) async-start(bf16[4,64,16,128]{3,1,0,2:T(8,128)(2,1)} %copy.29), calls=%async_computation.2 | async-start | bytes 2097152 | tf_op jit(solution)/shard_map/all_to_all | solution.py:66
  74.9 1.4 copy.47
  76.4 1.3 copy.31
  77.7 22.0 %all-to-all-done.2 = bf16[4,64,16,128]{3,1,0,2:T(8,128)(2,1)S(1)} async-done(((bf16[4,64,16,128]{3,1,0,2:T(8,128)(2,1)}), bf16[4,64,16,128]{3,1,0,2:T(8,128)(2,1)S(1)}, u32[]{:S(2)}, u32[]{:S(2)}) %all-to-all-start.2) | async-done | bytes 1048608 | tf_op jit(solution)/shard_map/all_to_all | solution.py:66
  99.7 6.7 %all-to-all-start.3 = ((bf16[4,64,16,128]{3,1,0,2:T(8,128)(2,1)}), bf16[4,64,16,128]{3,1,0,2:T(8,128)(2,1)}, u32[]{:S(2)}, u32[]{:S(2)}) async-start(bf16[4,64,16,128]{3,1,0,2:T(8,128)(2,1)} %copy.31), calls=%async_computation.3 | async-start | bytes 2097152 | tf_op jit(solution)/shard_map/all_to_all | solution.py:65
  106.7 1.0 copy-done.1
  107.8 23.5 %all-to-all-done.3 = bf16[4,64,16,128]{3,1,0,2:T(8,128)(2,1)} async-done(((bf16[4,64,16,128]{3,1,0,2:T(8,128)(2,1)}), bf16[4,64,16,128]{3,1,0,2:T(8,128)(2,1)}, u32[]{:S(2)}, u32[]{:S(2)}) %all-to-all-start.3) | async-done | bytes 1048608 | tf_op jit(solution)/shard_map/all_to_all | solution.py:65
  131.3 2.3 copy.32
  133.6 44.2 %while.18 = (s32[]{:T(128)}, bf16[4,1,1024,128]{3,2,1,0:T(8,128)(2,1)}, bf16[4,1,1024,128]{3,2,1,0:T(8,128)(2,1)}, bf16[4,1,1024,128]{3,2,1,0:T(8,128)(2,1)}, f3...) while((s32[]{:T(128)}, ...), condition=%wide.region_10.11_spmd, body=%wide.region_0.10_spmd.sunk | while | flops 1370094592 | bytes 42093704 | solution.py:69
  134.0 0.8 multiply_reduce_fusion.4
  135.6 1.6 fusion.102
  137.2 2.0 multiply_reduce_fusion.5
  139.3 1.2 multiply_convert_fusion.2
  140.5 0.9 fusion.100
  141.4 1.1 fusion.101
  142.4 1.2 fusion.98
  143.6 1.1 fusion.99
  145.0 0.8 multiply_reduce_fusion.4
  145.9 0.7 fusion.97
  146.6 1.6 fusion.102
  148.3 2.0 multiply_reduce_fusion.5
  150.3 1.2 multiply_convert_fusion.2
  151.5 0.9 fusion.100
  152.4 1.1 fusion.101
  153.5 1.2 fusion.98
  154.6 1.1 fusion.99
  156.1 0.8 multiply_reduce_fusion.4
  157.7 1.6 fusion.102
  159.3 2.0 multiply_reduce_fusion.5
  161.4 1.2 multiply_convert_fusion.2
  162.6 0.9 fusion.100
  163.5 1.1 fusion.101
  164.5 1.1 fusion.98
  165.7 1.1 fusion.99
  167.1 0.8 multiply_reduce_fusion.4
  168.7 1.6 fusion.102
  170.4 2.0 multiply_reduce_fusion.5
  172.4 1.2 multiply_convert_fusion.2
  173.6 0.9 fusion.100
  174.5 1.1 fusion.101
  175.6 1.2 fusion.98
  176.7 1.1 fusion.99
  177.8 3.2 %copy.53 = bf16[4,1,1024,128]{3,0,2,1:T(4,128)(2,1)} copy(bf16[4,1,1024,128]{3,2,1,0:T(8,128)(2,1)} %get-tuple-element.70) | data formatting | bytes 2097152 | tf_op jit(solution)/shard_map/while | solution.py:69
  181.0 6.7 %all-to-all-start.4 = ((bf16[4,1024,1,128]{3,0,2,1:T(4,128)(2,1)}), bf16[4,1024,1,128]{3,0,2,1:T(4,128)(2,1)S(1)}, u32[]{:S(2)}, u32[]{:S(2)}) async-start(bf16[4,1024,1,128]{3,0,2,1:T(4,128)(2,1)} %bitcast.188), calls=%async_computation.4 | async-start | bytes 2097152 | tf_op jit(solution)/shard_map/all_to_all | solution.py:74
  187.7 1.8 copy.52
  189.5 23.0 %all-to-all-done.4 = bf16[4,1024,1,128]{3,0,2,1:T(4,128)(2,1)S(1)} async-done(((bf16[4,1024,1,128]{3,0,2,1:T(4,128)(2,1)}), bf16[4,1024,1,128]{3,0,2,1:T(4,128)(2,1)S(1)}, u32[]{:S(2)}, u32[]{:S(2)}) %all-to-all-start.4) | async-done | bytes 1048608 | tf_op jit(solution)/shard_map/all_to_all | solution.py:74
  212.4 6.7 %all-to-all-start.5 = ((bf16[4,1024,1,128]{3,0,2,1:T(4,128)(2,1)}), bf16[4,1024,1,128]{3,0,2,1:T(4,128)(2,1)S(1)}, u32[]{:S(2)}, u32[]{:S(2)}) async-start(bf16[4,1024,1,128]{3,0,2,1:T(4,128)(2,1)} %bitcast.187), calls=%async_computation.5 | async-start | bytes 2097152 | tf_op jit(solution)/shard_map/all_to_all | solution.py:75
  219.2 1.8 copy.51
  221.0 22.9 %all-to-all-done.5 = bf16[4,1024,1,128]{3,0,2,1:T(4,128)(2,1)S(1)} async-done(((bf16[4,1024,1,128]{3,0,2,1:T(4,128)(2,1)}), bf16[4,1024,1,128]{3,0,2,1:T(4,128)(2,1)S(1)}, u32[]{:S(2)}, u32[]{:S(2)}) %all-to-all-start.5) | async-done | bytes 1048608 | tf_op jit(solution)/shard_map/all_to_all | solution.py:75
  243.9 6.7 %all-to-all-start.6 = ((bf16[4,1024,1,128]{3,0,2,1:T(4,128)(2,1)}), bf16[4,1024,1,128]{3,0,2,1:T(4,128)(2,1)S(1)}, u32[]{:S(2)}, u32[]{:S(2)}) async-start(bf16[4,1024,1,128]{3,0,2,1:T(4,128)(2,1)} %bitcast.186), calls=%async_computation.6 | async-start | bytes 2097152 | tf_op jit(solution)/shard_map/all_to_all | solution.py:76
  250.7 41.2 %psum.7 = f32[2,1,128]{2,0,1:T(2,128)} all-reduce(f32[2,1,128]{2,0,1:T(2,128)S(1)} %maximum_bitcast_fusion), channel_id=1, replica_groups=mesh['clip'=2,'patch'=16,'frame'=8] {'clip','frame'}, use_global_device_ids=true, to_apply=%region_13.14 | all-reduce | flops 256 | bytes 2048 | tf_op jit(solution)/shard_map/psum | solution.py:81
  291.9 1.6 copy.38
  293.5 2.3 reshape.322
  296.5 1.3 reshape.324
  298.5 1.3 reshape.326
  (63 shorter events, 5.7 us)
Async XLA Ops:
  0.6 11.4 %copy-start.2 = (bf16[2,2,64,2048]{3,2,1,0:T(8,128)(2,1)S(1)}, bf16[2,2,64,2048]{3,2,1,0:T(8,128)(2,1)}, u32[]{:S(2)}) copy-start(bf16[2,2,64,2048]{3,2,1,0:T(8,128)(2,1)} %param.9) | copy-start | bytes 3145732
  3.4 33.3 %all-to-all-start = ((bf16[4,64,16,128]{3,1,0,2:T(8,128)(2,1)}), bf16[4,64,16,128]{3,1,0,2:T(8,128)(2,1)S(1)}, u32[]{:S(2)}, u32[]{:S(2)}) async-start(bf16[4,64,16,128]{3,1,0,2:T(8,128)(2,1)} %copy.25), calls=%async_computation | async-start | bytes 2097152 | tf_op jit(solution)/shard_map/all_to_all | solution.py:63
  36.8 31.5 %all-to-all-start.1 = ((bf16[4,64,16,128]{3,1,0,2:T(8,128)(2,1)}), bf16[4,64,16,128]{3,1,0,2:T(8,128)(2,1)S(1)}, u32[]{:S(2)}, u32[]{:S(2)}) async-start(bf16[4,64,16,128]{3,1,0,2:T(8,128)(2,1)} %copy.27), calls=%async_computation.1 | async-start | bytes 2097152 | tf_op jit(solution)/shard_map/all_to_all | solution.py:64
  68.2 31.5 %all-to-all-start.2 = ((bf16[4,64,16,128]{3,1,0,2:T(8,128)(2,1)}), bf16[4,64,16,128]{3,1,0,2:T(8,128)(2,1)S(1)}, u32[]{:S(2)}, u32[]{:S(2)}) async-start(bf16[4,64,16,128]{3,1,0,2:T(8,128)(2,1)} %copy.29), calls=%async_computation.2 | async-start | bytes 2097152 | tf_op jit(solution)/shard_map/all_to_all | solution.py:66
  99.7 6.8 %copy-start = (bf16[4,64,16,128]{3,1,0,2:T(8,128)(2,1)}, bf16[4,64,16,128]{3,1,0,2:T(8,128)(2,1)S(1)}, u32[]{:S(2)}) copy-start(bf16[4,64,16,128]{3,1,0,2:T(8,128)(2,1)S(1)} %all-to-all-done.2) | copy-start | bytes 3145732
  99.7 31.6 %all-to-all-start.3 = ((bf16[4,64,16,128]{3,1,0,2:T(8,128)(2,1)}), bf16[4,64,16,128]{3,1,0,2:T(8,128)(2,1)}, u32[]{:S(2)}, u32[]{:S(2)}) async-start(bf16[4,64,16,128]{3,1,0,2:T(8,128)(2,1)} %copy.31), calls=%async_computation.3 | async-start | bytes 2097152 | tf_op jit(solution)/shard_map/all_to_all | solution.py:65
  106.4 1.2 copy-start.1
  106.5 27.1 %copy-start.5 = (f32[1,128]{1,0:T(1,128)S(1)}, f32[1,128]{1,0:T(1,128)}, u32[]{:S(2)}) copy-start(f32[1,128]{1,0:T(1,128)} %param.12) | copy-start | bytes 1540
  106.5 27.1 %copy-start.6 = (f32[1,128]{1,0:T(1,128)S(1)}, f32[1,128]{1,0:T(1,128)}, u32[]{:S(2)}) copy-start(f32[1,128]{1,0:T(1,128)} %param.13) | copy-start | bytes 1540
  177.8 9.9 %copy-start.3 = (bf16[4,1,1024,128]{3,2,1,0:T(8,128)(2,1)S(1)}, bf16[4,1,1024,128]{3,2,1,0:T(8,128)(2,1)}, u32[]{:S(2)}) copy-start(bf16[4,1,1024,128]{3,2,1,0:T(8,128)(2,1)} %get-tuple-element.71) | copy-start | bytes 3145732
  177.8 41.3 %copy-start.4 = (bf16[4,1,1024,128]{3,2,1,0:T(8,128)(2,1)S(1)}, bf16[4,1,1024,128]{3,2,1,0:T(8,128)(2,1)}, u32[]{:S(2)}) copy-start(bf16[4,1,1024,128]{3,2,1,0:T(8,128)(2,1)} %get-tuple-element.72) | copy-start | bytes 3145732
  181.0 31.5 %all-to-all-start.4 = ((bf16[4,1024,1,128]{3,0,2,1:T(4,128)(2,1)}), bf16[4,1024,1,128]{3,0,2,1:T(4,128)(2,1)S(1)}, u32[]{:S(2)}, u32[]{:S(2)}) async-start(bf16[4,1024,1,128]{3,0,2,1:T(4,128)(2,1)} %bitcast.188), calls=%async_computation.4 | async-start | bytes 2097152 | tf_op jit(solution)/shard_map/all_to_all | solution.py:74
  212.4 31.5 %all-to-all-start.5 = ((bf16[4,1024,1,128]{3,0,2,1:T(4,128)(2,1)}), bf16[4,1024,1,128]{3,0,2,1:T(4,128)(2,1)S(1)}, u32[]{:S(2)}, u32[]{:S(2)}) async-start(bf16[4,1024,1,128]{3,0,2,1:T(4,128)(2,1)} %bitcast.187), calls=%async_computation.5 | async-start | bytes 2097152 | tf_op jit(solution)/shard_map/all_to_all | solution.py:75
  243.9 53.9 %all-to-all-start.6 = ((bf16[4,1024,1,128]{3,0,2,1:T(4,128)(2,1)}), bf16[4,1024,1,128]{3,0,2,1:T(4,128)(2,1)S(1)}, u32[]{:S(2)}, u32[]{:S(2)}) async-start(bf16[4,1024,1,128]{3,0,2,1:T(4,128)(2,1)} %bitcast.186), calls=%async_computation.6 | async-start | bytes 2097152 | tf_op jit(solution)/shard_map/all_to_all | solution.py:76
where the time goes:
time: 301 us; the launch traced here: 300 us
  waiting for transfers between devices  137 us (46%)
  starting transfers between devices  48.8 us (16%)
  blocking collectives  41.2 us (14%)
  local copies, waits for them, and re-layouts  28 us (9%)
  matrix products  26.3 us (9%)
  other arithmetic  17.6 us (6%)
    psum x1, blocking collectives, body(): summed = lax.psum(partial_value, ('clip', 'frame'))  41.2 us
    all_to_all x1, waiting for transfers between devices, body(): lax.all_to_all(shaped[2], 'patch', split_axis=2, concat_axis=1, tiled=True)  23.5 us
    all_to_all x1, waiting for transfers between devices, body(): lax.all_to_all(shaped[0], 'patch', split_axis=2, concat_axis=1, tiled=True)  23.3 us
    all_to_all x1, waiting for transfers between devices, body(): lax.all_to_all(leaving[0], 'patch', split_axis=1, concat_axis=2, tiled=True)  23 us
    all_to_all x1, waiting for transfers between devices, body(): lax.all_to_all(leaving[1], 'patch', split_axis=1, concat_axis=2, tiled=True)  22.9 us
    all_to_all x1, waiting for transfers between devices, body(): lax.all_to_all(shaped[1], 'patch', split_axis=2, concat_axis=1, tiled=True)  22 us
    all_to_all x1, waiting for transfers between devices, body(): lax.all_to_all(shaped[3], 'patch', split_axis=2, concat_axis=1, tiled=True)  22 us
    all_to_all x1, starting transfers between devices, body(): lax.all_to_all(shaped[0], 'patch', split_axis=2, concat_axis=1, tiled=True)  8.59 us
  transfers between devices with their start and end apart: 7, of which 6 were waited for; matrix products, arithmetic and copies ran while one was open for 6% of the time, Pallas kernels for 0%

commit v1 on v0

v1 whole, which is shorter than its diff:
```python
import functools
import math

import jax
import jax.numpy as jnp
from jax import lax
from jax.experimental import pallas as pl
from jax.experimental.pallas import tpu as pltpu
from jax.sharding import PartitionSpec as P

EPS = 1e-06
HEADS = 16
DEPTH = 128
BLOCK = 256
CHUNKS = ((0, 1), (1, 2))
F32 = jnp.float32
BF16 = jnp.bfloat16


def pack_kernel(q_ref, k_ref, v_ref, g_ref, out_ref):
    for a, ref in enumerate((q_ref, k_ref, v_ref, g_ref)):
        for h in range(HEADS):
            out_ref[h, a, 0] = ref[0, 0, :, h * DEPTH : (h + 1) * DEPTH]


def pack(arrays, first, clips):
    _, frames, rows, width = arrays[0].shape
    items = clips * frames
    spec = pl.BlockSpec((1, 1, rows, width), lambda i: (first + i // frames, i % frames, 0, 0))
    return pl.pallas_call(
        pack_kernel,
        grid=(items,),
        in_specs=[spec] * 4,
        out_specs=pl.BlockSpec((HEADS, 4, 1, rows, DEPTH), lambda i: (0, 0, i, 0, 0)),
        out_shape=jax.ShapeDtypeStruct((HEADS, 4, items, rows, DEPTH), BF16),
        name="pack",
    )(*arrays)


def unpack_kernel(in_ref, *refs):
    for a, ref in enumerate(refs[-3:]):
        for h in range(HEADS):
            ref[0, 0, :, h * DEPTH : (h + 1) * DEPTH] = in_ref[h, a, 0]


def unpack(arrived, first, clips, shape, earlier):
    _, frames, rows, width = shape
    items = clips * frames
    spec = pl.BlockSpec((1, 1, rows, width), lambda i: (first + i // frames, i % frames, 0, 0))
    return pl.pallas_call(
        unpack_kernel,
        grid=(items,),
        in_specs=[pl.BlockSpec((HEADS, 3, 1, rows, DEPTH), lambda i: (0, 0, i, 0, 0))]
        + [pl.BlockSpec(memory_space=pl.ANY)] * len(earlier),
        out_specs=[spec] * 3,
        out_shape=[jax.ShapeDtypeStruct(shape, BF16)] * 3,
        input_output_aliases={1 + i: i for i in range(len(earlier))},
        name="unpack",
    )(arrived, *earlier)


def normalize(raw, gain):
    wide = raw.astype(F32)
    scale = lax.rsqrt(jnp.mean(wide * wide, axis=-1, keepdims=True) + EPS)
    unit = wide * scale
    return unit, scale, (unit * gain).astype(BF16)


def restore(grad_norm, unit, scale, gain):
    grad_unit = grad_norm * gain
    along = jnp.mean(grad_unit * unit, axis=-1, keepdims=True)
    return (scale * (grad_unit - unit * along)).astype(BF16), grad_norm * unit


def dot(a, b, dims):
    return lax.dot_general(a, b, (dims, ((), ())), preferred_element_type=F32)


def attend_kernel(in_ref, gain_q_ref, gain_k_ref, out_ref, gains_ref, gv_ref, gk_ref):
    sources, _, _, rows, depth = in_ref.shape
    total = sources * rows
    inverse = 1.0 / math.sqrt(depth)
    gain_q = gain_q_ref[...]
    gain_k = gain_k_ref[...]

    def whole(a):
        return in_ref[:, a, 0].reshape(total, depth)

    k_unit, k_scale, k_norm = normalize(whole(1), gain_k)
    values = whole(2)
    k_turned = k_norm.T
    each = BLOCK // rows
    term_q = jnp.zeros((1, depth), F32)
    for b in range(total // BLOCK):
        part = pl.ds(b * each, each)
        q_unit, q_scale, q_norm = normalize(in_ref[part, 0, 0].reshape(BLOCK, depth), gain_q)
        grad_out = in_ref[part, 3, 0].reshape(BLOCK, depth)
        scores = dot(k_norm, q_norm, ((1,), (1,)))
        top = jnp.max(scores, axis=0, keepdims=True)
        expo = jnp.exp((scores - top) * inverse)
        prob = expo * (1.0 / jnp.sum(expo, axis=0, keepdims=True))
        dprob = dot(values, grad_out, ((1,), (1,)))
        delta = jnp.sum(prob * dprob, axis=0, keepdims=True)
        dscore = (prob * (dprob - delta)).astype(BF16)
        grad_v = dot(prob.astype(BF16), grad_out, ((1,), (0,)))
        grad_k = dot(dscore, q_norm, ((1,), (0,)))
        if b == 0:
            gv_ref[...] = grad_v
            gk_ref[...] = grad_k
        else:
            gv_ref[...] += grad_v
            gk_ref[...] += grad_k
        grad_qn = dot(k_turned, dscore, ((1,), (0,))).T * inverse
        grad_q, term = restore(grad_qn, q_unit, q_scale, gain_q)
        out_ref[part, 0, 0] = grad_q.reshape(each, rows, depth)
        term_q += jnp.sum(term, axis=0, keepdims=True)
    grad_k, term = restore(gk_ref[...] * inverse, k_unit, k_scale, gain_k)
    out_ref[:, 1, 0] = grad_k.reshape(sources, rows, depth)
    out_ref[:, 2, 0] = gv_ref[...].astype(BF16).reshape(sources, rows, depth)
    gains_ref[0, 0:1] = term_q
    gains_ref[0, 1:2] = jnp.sum(term, axis=0, keepdims=True)


def attend(arrived, gain_q, gain_k):
    sources, _, items, rows, depth = arrived.shape
    total = sources * rows
    gain = pl.BlockSpec((1, depth), lambda i: (0, 0))
    return pl.pallas_call(
        attend_kernel,
        grid=(items,),
        in_specs=[
            pl.BlockSpec((sources, 4, 1, rows, depth), lambda i: (0, 0, i, 0, 0)),
            gain,
            gain,
        ],
        out_specs=[
            pl.BlockSpec((sources, 3, 1, rows, depth), lambda i: (0, 0, i, 0, 0)),
            pl.BlockSpec((1, 2, depth), lambda i: (i, 0, 0)),
        ],
        out_shape=[
            jax.ShapeDtypeStruct((sources, 3, items, rows, depth), BF16),
            jax.ShapeDtypeStruct((items, 2, depth), F32),
        ],
        scratch_shapes=[pltpu.VMEM((total, depth), F32)] * 2,
        compiler_params=pltpu.CompilerParams(vmem_limit_bytes=40 * 1024 * 1024),
        cost_estimate=pl.CostEstimate(
            flops=items * 10 * total * total * depth,
            bytes_accessed=items * total * depth * 14,
            transcendentals=items * total * total,
        ),
        name="attend",
    )(arrived, gain_q, gain_k)


def body(queries, keys, values, grad_out, gain_q, gain_k):
    arrays = (queries, keys, values, grad_out)
    exchange = functools.partial(
        lax.all_to_all, axis_name="patch", split_axis=0, concat_axis=0, tiled=True
    )
    arrived = [exchange(pack(arrays, first, last - first)) for first, last in CHUNKS]
    done = [attend(a, gain_q, gain_k) for a in arrived]
    grads = ()
    for (first, last), (leaving, _) in zip(CHUNKS, done):
        grads = unpack(exchange(leaving), first, last - first, queries.shape, grads)
    terms = sum(jnp.sum(gains, axis=0) for _, gains in done)
    gain_grads = lax.psum(terms, ("clip", "frame")).reshape(2, 1, DEPTH)
    return (*grads, gain_grads)


def solution(mesh):
    wide = P("clip", "frame", "patch", None)
    gain = P("patch", None)
    return jax.shard_map(
        body,
        mesh=mesh,
        in_specs=(wide, wide, wide, wide, gain, gain),
        out_specs=(wide, wide, wide, P(None, "patch", None)),
        check_vma=False,
    )
```

time: 301 us -> 212 us (0.70)
  waiting for transfers between devices: 137 us -> 103 us
  Pallas kernels: 0 us -> 31.2 us
  matrix products: 26.3 us -> 0 us
  local copies, waits for them, and re-layouts: 28 us -> 6.36 us
  starting transfers between devices: 48.8 us -> 28.3 us
  other arithmetic: 17.6 us -> 0.03 us
    all_to_all x7 -> x4, waiting for transfers between devices: 137 us -> 103 us  [the longest x2 78.8 us: body(): exchange(pack(arrays, first, last - first))]
    pallas_call x0 -> x6, Pallas kernels: none -> 31.2 us  [the longest x2 20.9 us: attend(): pl.pallas_call(attend_kernel, grid=(items,), in_specs=[pl.BlockSpec((sour...]
    dot_general x20 -> x0, matrix products: 26.3 us -> none  [the longest x4 8.18 us: frame_grads(): jnp.einsum('fpe,fke->fpk', grad_out, values, preferred_element_type=jnp.f...]
    all_to_all x7 -> x4, starting transfers between devices: 48.8 us -> 28.3 us  [the longest x2 15.1 us: body(): exchange(pack(arrays, first, last - first))]
    reshape x7 -> x0, local copies, waits for them, and re-layouts: 9.89 us -> none  [the longest x4 5.05 us: body(): a.reshape(count, rows, heads, depth)]
    dynamic_update_slice x8 -> x0, other arithmetic: 8.41 us -> none  [body(): lax.map(lambda items: frame_grads(items, gain_q, gain_k), local)]
    while x3 -> x0, local copies, waits for them, and re-layouts: 6.76 us -> none  [body(): lax.map(lambda items: frame_grads(items, gain_q, gain_k), local)]
    all_to_all x7 -> x0, local copies, waits for them, and re-layouts: 5.61 us -> none  [the longest x1 2.35 us: body(): lax.all_to_all(shaped[2], 'patch', split_axis=2, concat_axis=1, tiled=True)]
  transfers between devices with their start and end apart: 7 -> 4, of which waited for: 6 -> 3; matrix products, arithmetic and copies ran while one was open for 6% -> 0% of each run, Pallas kernels for 0% -> 12%
where the time goes in v1:
time: 212 us; the launch traced here: 211 us
  waiting for transfers between devices  103 us (49%)
  blocking collectives  41.2 us (19%)
  Pallas kernels  31.2 us (15%)
  starting transfers between devices  28.3 us (13%)
  local copies, waits for them, and re-layouts  6.36 us (3%)
    all_to_all x2, waiting for transfers between devices, body(): exchange(pack(arrays, first, last - first))  78.8 us
    psum x1, blocking collectives, body(): gain_grads = lax.psum(terms, ('clip', 'frame')).reshape(2, 1, DEPTH)  41.2 us
    all_to_all x2, waiting for transfers between devices, body(): grads = unpack(exchange(leaving), first, last - first, queries.shape, grads)  24.6 us
    pallas_call x2, Pallas kernels, attend(): pl.pallas_call(attend_kernel, grid=(items,), in_specs=[pl.BlockSpec((sour...  20.9 us
    all_to_all x2, starting transfers between devices, body(): exchange(pack(arrays, first, last - first))  15.1 us
    all_to_all x2, starting transfers between devices, body(): grads = unpack(exchange(leaving), first, last - first, queries.shape, grads)  13.2 us
    unnamed x14, local copies, waits for them, and re-layouts  6.36 us
    pallas_call x2, Pallas kernels, pack(): pl.pallas_call(pack_kernel, grid=(items,), in_specs=[spec] * 4, out_specs...  5.48 us
  transfers between devices with their start and end apart: 4, of which 3 were waited for; matrix products, arithmetic and copies ran while one was open for 0% of the time, Pallas kernels for 12%

profile of v1, /device:TPU:32, one launch (start us, length us, event | category | flops | bytes accessed | tf_op | source)
XLA Modules:
  0.0 211.2 jit_solution(6988194908152785019)
XLA Ops:
  0.6 2.8 %pack.3 = bf16[16,4,2,64,128]{4,3,2,1,0:T(8,128)(2,1)} custom-call(bf16[2,2,64,2048]{3,2,1,0:T(8,128)(2,1)} %q_ref.3, bf16[2,2,64,2048]{3,2,1,0:T(8,128)(2,1)} %k_ref.3, bf16[2,2,64,2048]{3,2,1,0:T(8,128)(2,1)} %v_ref.3, bf16[2,2,64,2048]{3,2,1,0:T(8,128)(2,1)} %g_ref.3), custom_call_target="tpu_custom_call" | custom-call | tf_op jit(solution)/shard_map/pack/pallas_call | solution.py:30
  3.4 8.6 %all-to-all-start.2 = ((bf16[16,4,2,64,128]{4,3,2,1,0:T(8,128)(2,1)}), bf16[16,4,2,64,128]{4,3,2,1,0:T(8,128)(2,1)S(1)}, u32[]{:S(2)}, u32[]{:S(2)}) async-start(bf16[16,4,2,64,128]{4,3,2,1,0:T(8,128)(2,1)} %pack.3), calls=%async_computation.2 | async-start | bytes 4194304 | tf_op jit(solution)/shard_map/all_to_all | solution.py:160
  12.0 2.7 %pack.2 = bf16[16,4,2,64,128]{4,3,2,1,0:T(8,128)(2,1)} custom-call(bf16[2,2,64,2048]{3,2,1,0:T(8,128)(2,1)} %q_ref.3, bf16[2,2,64,2048]{3,2,1,0:T(8,128)(2,1)} %k_ref.3, bf16[2,2,64,2048]{3,2,1,0:T(8,128)(2,1)} %v_ref.3, bf16[2,2,64,2048]{3,2,1,0:T(8,128)(2,1)} %g_ref.3), custom_call_target="tpu_custom_call" | custom-call | tf_op jit(solution)/shard_map/pack/pallas_call | solution.py:30
  14.7 0.0 copy-start.4
  14.7 0.0 copy-start.5
  14.7 44.7 %all-to-all-done.2.in_ref = bf16[16,4,2,64,128]{4,3,2,1,0:T(8,128)(2,1)S(1)} async-done(((bf16[16,4,2,64,128]{4,3,2,1,0:T(8,128)(2,1)}), bf16[16,4,2,64,128]{4,3,2,1,0:T(8,128)(2,1)S(1)}, u32[]{:S(2)}, u32[]{:S(2)}) %all-to-all-start.2) | async-done | bytes 2097184 | tf_op jit(solution)/shard_map/all_to_all | solution.py:160
  59.4 0.0 copy-start
  59.4 1.3 copy-done
  60.7 6.5 %all-to-all-start = ((bf16[16,4,2,64,128]{4,3,2,1,0:T(8,128)(2,1)}), bf16[16,4,2,64,128]{4,3,2,1,0:T(8,128)(2,1)S(1)}, u32[]{:S(2)}, u32[]{:S(2)}) async-start(bf16[16,4,2,64,128]{4,3,2,1,0:T(8,128)(2,1)} %pack.2), calls=%async_computation | async-start | bytes 4194304 | tf_op jit(solution)/shard_map/all_to_all | solution.py:160
  67.2 0.0 copy-done.4
  67.2 0.0 copy-done.5
  67.2 0.0 copy-start.1
  67.3 1.6 copy-done.1
  68.8 10.4 %attend.3 = (bf16[16,3,2,64,128]{4,3,2,1,0:T(8,128)(2,1)S(1)}, f32[2,2,128]{2,1,0:T(2,128)S(1)}) custom-call(bf16[16,4,2,64,128]{4,3,2,1,0:T(8,128)(2,1)S(1)} %copy-done.1, f32[1,128]{1,0:T(1,128)S(1)} %copy-done.4, f32[1,128]{1,0:T(1,128)S(1)} %copy-done.5), custom_call_target="tpu_custom_call" | custom-call | flops 2684354560 | bytes 3670016 | tf_op jit(solution)/shard_map/attend/pallas_call | solution.py:128
  79.3 0.0 copy-start.3
  79.3 1.2 copy-done.3
  80.5 34.1 %all-to-all-done.in_ref = bf16[16,4,2,64,128]{4,3,2,1,0:T(8,128)(2,1)S(1)} async-done(((bf16[16,4,2,64,128]{4,3,2,1,0:T(8,128)(2,1)}), bf16[16,4,2,64,128]{4,3,2,1,0:T(8,128)(2,1)S(1)}, u32[]{:S(2)}, u32[]{:S(2)}) %all-to-all-start) | async-done | bytes 2097184 | tf_op jit(solution)/shard_map/all_to_all | solution.py:160
  114.6 6.5 %all-to-all-start.3 = ((bf16[16,3,2,64,128]{4,3,2,1,0:T(8,128)(2,1)}), bf16[16,3,2,64,128]{4,3,2,1,0:T(8,128)(2,1)}, u32[]{:S(2)}, u32[]{:S(2)}) async-start(bf16[16,3,2,64,128]{4,3,2,1,0:T(8,128)(2,1)} %copy-done.3), calls=%async_computation.3 | async-start | bytes 3145728 | tf_op jit(solution)/shard_map/all_to_all | solution.py:164
  121.2 10.4 %attend.2 = (bf16[16,3,2,64,128]{4,3,2,1,0:T(8,128)(2,1)S(1)}, f32[2,2,128]{2,1,0:T(2,128)S(1)}) custom-call(bf16[16,4,2,64,128]{4,3,2,1,0:T(8,128)(2,1)S(1)} %all-to-all-done.in_ref, f32[1,128]{1,0:T(1,128)S(1)} %copy-done.4, f32[1,128]{1,0:T(1,128)S(1)} %copy-done.5), custom_call_target="tpu_custom_call" | custom-call | flops 2684354560 | bytes 3670016 | tf_op jit(solution)/shard_map/attend/pallas_call | solution.py:128
  131.6 0.0 copy-start.2
  131.6 1.1 copy-done.2
  132.8 24.6 %all-to-all-done.3.in_ref = bf16[16,3,2,64,128]{4,3,2,1,0:T(8,128)(2,1)} async-done(((bf16[16,3,2,64,128]{4,3,2,1,0:T(8,128)(2,1)}), bf16[16,3,2,64,128]{4,3,2,1,0:T(8,128)(2,1)}, u32[]{:S(2)}, u32[]{:S(2)}) %all-to-all-start.3) | async-done | bytes 1572896 | tf_op jit(solution)/shard_map/all_to_all | solution.py:164
  157.3 6.6 %all-to-all-start.1 = ((bf16[16,3,2,64,128]{4,3,2,1,0:T(8,128)(2,1)}), bf16[16,3,2,64,128]{4,3,2,1,0:T(8,128)(2,1)S(1)}, u32[]{:S(2)}, u32[]{:S(2)}) async-start(bf16[16,3,2,64,128]{4,3,2,1,0:T(8,128)(2,1)} %copy-done.2), calls=%async_computation.1 | async-start | bytes 3145728 | tf_op jit(solution)/shard_map/all_to_all | solution.py:164
  164.0 41.2 %psum.7 = f32[2,1,128]{2,1,0:T(1,128)} all-reduce(f32[2,1,128]{2,1,0:T(1,128)S(1)} %bitcast.1), channel_id=1, replica_groups=mesh['clip'=2,'patch'=16,'frame'=8] {'clip','frame'}, use_global_device_ids=true, to_apply=%region_2.0 | all-reduce | flops 256 | bytes 2048 | tf_op jit(solution)/shard_map/psum | solution.py:166
  205.2 2.4 %unpack.2 = (bf16[2,2,64,2048]{3,2,1,0:T(8,128)(2,1)}, bf16[2,2,64,2048]{3,2,1,0:T(8,128)(2,1)}, bf16[2,2,64,2048]{3,2,1,0:T(8,128)(2,1)}) custom-call(bf16[16,3,2,64,128]{4,3,2,1,0:T(8,128)(2,1)} %all-to-all-done.3.in_ref), custom_call_target="tpu_custom_call" | custom-call | tf_op jit(solution)/shard_map/unpack/pallas_call | solution.py:50
  207.6 0.0 all-to-all-done.1.in_ref
  207.6 0.0 copy-start.6
  207.6 1.2 copy-done.6
  208.8 2.4 %unpack.3 = (bf16[2,2,64,2048]{3,2,1,0:T(8,128)(2,1)}, bf16[2,2,64,2048]{3,2,1,0:T(8,128)(2,1)}, bf16[2,2,64,2048]{3,2,1,0:T(8,128)(2,1)}) custom-call(bf16[16,3,2,64,128]{4,3,2,1,0:T(8,128)(2,1)} %copy-done.6, bf16[2,2,64,2048]{3,2,1,0:T(8,128)(2,1)} %get-tuple-element.16.refs_0_, ...), custom_call_target="tpu_custom_call", output_to_operand_aliasing={{0}: (1, {}), {1}: (2, {}), {2}: (3, {})} | custom-call | tf_op jit(solution)/shard_map/unpack/pallas_call | solution.py:50
  (3 shorter events, 0.0 us)
Async XLA Ops:
  3.4 56.0 %all-to-all-start.2 = ((bf16[16,4,2,64,128]{4,3,2,1,0:T(8,128)(2,1)}), bf16[16,4,2,64,128]{4,3,2,1,0:T(8,128)(2,1)S(1)}, u32[]{:S(2)}, u32[]{:S(2)}) async-start(bf16[16,4,2,64,128]{4,3,2,1,0:T(8,128)(2,1)} %pack.3), calls=%async_computation.2 | async-start | bytes 4194304 | tf_op jit(solution)/shard_map/all_to_all | solution.py:160
  14.7 52.5 %copy-start.4 = (f32[1,128]{1,0:T(1,128)S(1)}, f32[1,128]{1,0:T(1,128)}, u32[]{:S(2)}) copy-start(f32[1,128]{1,0:T(1,128)} %gain_q_ref.3) | copy-start | bytes 1540
  14.7 52.5 %copy-start.5 = (f32[1,128]{1,0:T(1,128)S(1)}, f32[1,128]{1,0:T(1,128)}, u32[]{:S(2)}) copy-start(f32[1,128]{1,0:T(1,128)} %gain_k_ref.3) | copy-start | bytes 1540
  59.4 1.3 copy-start
  60.7 53.9 %all-to-all-start = ((bf16[16,4,2,64,128]{4,3,2,1,0:T(8,128)(2,1)}), bf16[16,4,2,64,128]{4,3,2,1,0:T(8,128)(2,1)S(1)}, u32[]{:S(2)}, u32[]{:S(2)}) async-start(bf16[16,4,2,64,128]{4,3,2,1,0:T(8,128)(2,1)} %pack.2), calls=%async_computation | async-start | bytes 4194304 | tf_op jit(solution)/shard_map/all_to_all | solution.py:160
  67.2 1.6 copy-start.1
  79.3 1.2 copy-start.3
  114.6 42.7 %all-to-all-start.3 = ((bf16[16,3,2,64,128]{4,3,2,1,0:T(8,128)(2,1)}), bf16[16,3,2,64,128]{4,3,2,1,0:T(8,128)(2,1)}, u32[]{:S(2)}, u32[]{:S(2)}) async-start(bf16[16,3,2,64,128]{4,3,2,1,0:T(8,128)(2,1)} %copy-done.3), calls=%async_computation.3 | async-start | bytes 3145728 | tf_op jit(solution)/shard_map/all_to_all | solution.py:164
  131.6 1.1 copy-start.2
  157.3 50.3 %all-to-all-start.1 = ((bf16[16,3,2,64,128]{4,3,2,1,0:T(8,128)(2,1)}), bf16[16,3,2,64,128]{4,3,2,1,0:T(8,128)(2,1)S(1)}, u32[]{:S(2)}, u32[]{:S(2)}) async-start(bf16[16,3,2,64,128]{4,3,2,1,0:T(8,128)(2,1)} %copy-done.2), calls=%async_computation.1 | async-start | bytes 3145728 | tf_op jit(solution)/shard_map/all_to_all | solution.py:164
  207.6 1.2 copy-start.6

commit v2 on v1

--- a/solution.py
+++ b/solution.py
@@ -12,6 +12,7 @@
 HEADS = 16
 DEPTH = 128
 BLOCK = 256
+VMEM_LIMIT = 63 * 1024 * 1024
 CHUNKS = ((0, 1), (1, 2))
 F32 = jnp.float32
 BF16 = jnp.bfloat16
@@ -33,6 +34,7 @@
         in_specs=[spec] * 4,
         out_specs=pl.BlockSpec((HEADS, 4, 1, rows, DEPTH), lambda i: (0, 0, i, 0, 0)),
         out_shape=jax.ShapeDtypeStruct((HEADS, 4, items, rows, DEPTH), BF16),
+        compiler_params=pltpu.CompilerParams(vmem_limit_bytes=VMEM_LIMIT),
         name="pack",
     )(*arrays)
 
@@ -55,6 +57,7 @@
         out_specs=[spec] * 3,
         out_shape=[jax.ShapeDtypeStruct(shape, BF16)] * 3,
         input_output_aliases={1 + i: i for i in range(len(earlier))},
+        compiler_params=pltpu.CompilerParams(vmem_limit_bytes=VMEM_LIMIT),
         name="unpack",
     )(arrived, *earlier)
 
@@ -97,7 +100,7 @@
         grad_out = in_ref[part, 3, 0].reshape(BLOCK, depth)
         scores = dot(k_norm, q_norm, ((1,), (1,)))
         top = jnp.max(scores, axis=0, keepdims=True)
-        expo = jnp.exp((scores - top) * inverse)
+        expo = jnp.exp2((scores - top) * (inverse * math.log2(math.e)))
         prob = expo * (1.0 / jnp.sum(expo, axis=0, keepdims=True))
         dprob = dot(values, grad_out, ((1,), (1,)))
         delta = jnp.sum(prob * dprob, axis=0, keepdims=True)
@@ -142,7 +145,7 @@
             jax.ShapeDtypeStruct((items, 2, depth), F32),
         ],
         scratch_shapes=[pltpu.VMEM((total, depth), F32)] * 2,
-        compiler_params=pltpu.CompilerParams(vmem_limit_bytes=40 * 1024 * 1024),
+        compiler_params=pltpu.CompilerParams(vmem_limit_bytes=VMEM_LIMIT),
         cost_estimate=pl.CostEstimate(
             flops=items * 10 * total * total * depth,
             bytes_accessed=items * total * depth * 14,
@@ -150,6 +153,15 @@
         ),
         name="attend",
     )(arrived, gain_q, gain_k)
+
+
+def total_of(x):
+    for axis in ("clip", "frame"):
+        size, step = lax.axis_size(axis), 1
+        while step < size:
+            x = x + lax.ppermute(x, axis, [(i, i ^ step) for i in range(size)])
+            step *= 2
+    return x
 
 
 def body(queries, keys, values, grad_out, gain_q, gain_k):
@@ -163,7 +175,7 @@
     for (first, last), (leaving, _) in zip(CHUNKS, done):
         grads = unpack(exchange(leaving), first, last - first, queries.shape, grads)
     terms = sum(jnp.sum(gains, axis=0) for _, gains in done)
-    gain_grads = lax.psum(terms, ("clip", "frame")).reshape(2, 1, DEPTH)
+    gain_grads = total_of(terms).reshape(2, 1, DEPTH)
     return (*grads, gain_grads)
 
 

time: 212 us -> 206 us (0.972)
  the two profiles are of different devices: /device:TPU:32 before, /device:TPU:1 now
where the time goes in v2:
time: 206 us; the launch traced here: 205 us
  waiting for transfers between devices  137 us (67%)
  Pallas kernels  34.6 us (17%)
  starting transfers between devices  32.5 us (16%)
    all_to_all x2, waiting for transfers between devices, body(): exchange(pack(arrays, first, last - first))  83.2 us
    all_to_all x2, waiting for transfers between devices, body(): grads = unpack(exchange(leaving), first, last - first, queries.shape, grads)  48.6 us
    pallas_call x2, Pallas kernels, attend(): pl.pallas_call(attend_kernel, grid=(items,), in_specs=[pl.BlockSpec((sour...  24.3 us
    all_to_all x2, starting transfers between devices, body(): exchange(pack(arrays, first, last - first))  15 us
    all_to_all x2, starting transfers between devices, body(): grads = unpack(exchange(leaving), first, last - first, queries.shape, grads)  9.29 us
    ppermute x4, starting transfers between devices, total_of(): x = x + lax.ppermute(x, axis, [(i, i ^ step) for i in range(size)])  8.27 us
    pallas_call x2, Pallas kernels, pack(): pl.pallas_call(pack_kernel, grid=(items,), in_specs=[spec] * 4, out_specs...  5.48 us
    ppermute x4, waiting for transfers between devices, total_of(): x = x + lax.ppermute(x, axis, [(i, i ^ step) for i in range(size)])  4.92 us
  transfers between devices with their start and end apart: 8, of which 8 were waited for; matrix products, arithmetic and copies ran while one was open for 0% of the time, Pallas kernels for 14%

profile of v2, /device:TPU:1, one launch (start us, length us, event | category | flops | bytes accessed | tf_op | source)
XLA Modules:
  0.0 205.2 jit_solution(15549219544974735728)
XLA Ops:
  0.6 2.7 %pack.3 = bf16[16,4,2,64,128]{4,3,2,1,0:T(8,128)(2,1)} custom-call(bf16[2,2,64,2048]{3,2,1,0:T(8,128)(2,1)} %q_ref.3, bf16[2,2,64,2048]{3,2,1,0:T(8,128)(2,1)} %k_ref.3, bf16[2,2,64,2048]{3,2,1,0:T(8,128)(2,1)} %v_ref.3, bf16[2,2,64,2048]{3,2,1,0:T(8,128)(2,1)} %g_ref.3), custom_call_target="tpu_custom_call" | custom-call | tf_op jit(solution)/shard_map/pack/pallas_call | solution.py:31
  3.4 10.0 %all-to-all-start.2 = ((bf16[16,4,2,64,128]{4,3,2,1,0:T(8,128)(2,1)}), bf16[16,4,2,64,128]{4,3,2,1,0:T(8,128)(2,1)}, u32[]{:S(2)}, u32[]{:S(2)}) async-start(bf16[16,4,2,64,128]{4,3,2,1,0:T(8,128)(2,1)} %pack.3), calls=%async_computation.2 | async-start | bytes 4194304 | tf_op jit(solution)/shard_map/all_to_all | solution.py:172
  13.3 2.8 %pack.2 = bf16[16,4,2,64,128]{4,3,2,1,0:T(8,128)(2,1)} custom-call(bf16[2,2,64,2048]{3,2,1,0:T(8,128)(2,1)} %q_ref.3, bf16[2,2,64,2048]{3,2,1,0:T(8,128)(2,1)} %k_ref.3, bf16[2,2,64,2048]{3,2,1,0:T(8,128)(2,1)} %v_ref.3, bf16[2,2,64,2048]{3,2,1,0:T(8,128)(2,1)} %g_ref.3), custom_call_target="tpu_custom_call" | custom-call | tf_op jit(solution)/shard_map/pack/pallas_call | solution.py:31
  16.1 46.3 %all-to-all-done.2.in_ref = bf16[16,4,2,64,128]{4,3,2,1,0:T(8,128)(2,1)} async-done(((bf16[16,4,2,64,128]{4,3,2,1,0:T(8,128)(2,1)}), bf16[16,4,2,64,128]{4,3,2,1,0:T(8,128)(2,1)}, u32[]{:S(2)}, u32[]{:S(2)}) %all-to-all-start.2) | async-done | bytes 2097184 | tf_op jit(solution)/shard_map/all_to_all | solution.py:172
  62.4 5.0 %all-to-all-start = ((bf16[16,4,2,64,128]{4,3,2,1,0:T(8,128)(2,1)}), bf16[16,4,2,64,128]{4,3,2,1,0:T(8,128)(2,1)}, u32[]{:S(2)}, u32[]{:S(2)}) async-start(bf16[16,4,2,64,128]{4,3,2,1,0:T(8,128)(2,1)} %pack.2), calls=%async_computation | async-start | bytes 4194304 | tf_op jit(solution)/shard_map/all_to_all | solution.py:172
  67.4 12.2 %attend.3 = (bf16[16,3,2,64,128]{4,3,2,1,0:T(8,128)(2,1)}, f32[2,2,128]{2,1,0:T(2,128)}) custom-call(bf16[16,4,2,64,128]{4,3,2,1,0:T(8,128)(2,1)} %all-to-all-done.2.in_ref, f32[1,128]{1,0:T(1,128)} %gain_q_ref.3, f32[1,128]{1,0:T(1,128)} %gain_k_ref.3), custom_call_target="tpu_custom_call" | custom-call | flops 2684354560 | bytes 3670016 | tf_op jit(solution)/shard_map/attend/pallas_call | solution.py:131
  79.5 36.9 %all-to-all-done.in_ref = bf16[16,4,2,64,128]{4,3,2,1,0:T(8,128)(2,1)} async-done(((bf16[16,4,2,64,128]{4,3,2,1,0:T(8,128)(2,1)}), bf16[16,4,2,64,128]{4,3,2,1,0:T(8,128)(2,1)}, u32[]{:S(2)}, u32[]{:S(2)}) %all-to-all-start) | async-done | bytes 2097184 | tf_op jit(solution)/shard_map/all_to_all | solution.py:172
  116.4 5.0 %all-to-all-start.3 = ((bf16[16,3,2,64,128]{4,3,2,1,0:T(8,128)(2,1)}), bf16[16,3,2,64,128]{4,3,2,1,0:T(8,128)(2,1)}, u32[]{:S(2)}, u32[]{:S(2)}) async-start(bf16[16,3,2,64,128]{4,3,2,1,0:T(8,128)(2,1)} %get-tuple-element.15), calls=%async_computation.3 | async-start | bytes 3145728 | tf_op jit(solution)/shard_map/all_to_all | solution.py:176
  121.4 12.2 %attend.2 = (bf16[16,3,2,64,128]{4,3,2,1,0:T(8,128)(2,1)}, f32[2,2,128]{2,1,0:T(2,128)}) custom-call(bf16[16,4,2,64,128]{4,3,2,1,0:T(8,128)(2,1)} %all-to-all-done.in_ref, f32[1,128]{1,0:T(1,128)} %gain_q_ref.3, f32[1,128]{1,0:T(1,128)} %gain_k_ref.3), custom_call_target="tpu_custom_call" | custom-call | flops 2684354560 | bytes 3670016 | tf_op jit(solution)/shard_map/attend/pallas_call | solution.py:131
  133.6 0.0 copy-start
  133.6 0.0 copy-start.1
  133.6 26.4 %all-to-all-done.3.in_ref = bf16[16,3,2,64,128]{4,3,2,1,0:T(8,128)(2,1)} async-done(((bf16[16,3,2,64,128]{4,3,2,1,0:T(8,128)(2,1)}), bf16[16,3,2,64,128]{4,3,2,1,0:T(8,128)(2,1)}, u32[]{:S(2)}, u32[]{:S(2)}) %all-to-all-start.3) | async-done | bytes 1572896 | tf_op jit(solution)/shard_map/all_to_all | solution.py:176
  159.9 4.3 %all-to-all-start.1 = ((bf16[16,3,2,64,128]{4,3,2,1,0:T(8,128)(2,1)}), bf16[16,3,2,64,128]{4,3,2,1,0:T(8,128)(2,1)}, u32[]{:S(2)}, u32[]{:S(2)}) async-start(bf16[16,3,2,64,128]{4,3,2,1,0:T(8,128)(2,1)} %get-tuple-element.14), calls=%async_computation.1 | async-start | bytes 3145728 | tf_op jit(solution)/shard_map/all_to_all | solution.py:176
  164.3 0.0 copy-done
  164.3 0.0 copy-done.1
  164.3 1.4 collective-permute-start
  165.7 1.1 collective-permute-done
  166.9 1.2 collective-permute-start.1
  168.1 1.2 collective-permute-done.1
  169.3 2.7 %collective-permute-start.2 = (f32[2,128]{1,0:T(2,128)S(1)}, f32[2,128]{1,0:T(2,128)S(1)}, u32[]{:S(2)}, u32[]{:S(2)}) collective-permute-start(f32[2,128]{1,0:T(2,128)S(1)} %add.17), channel_id=1, source_target_pairs={{0,2},{1,3},{2,0},{3,1},{4,6},{5,7},{6,4},{7,5},{8,10},{9,11},{10,... | collective-permute-start | bytes 3080 | tf_op jit(solution)/shard_map/ppermute | solution.py:162
  172.0 1.2 collective-permute-done.2
  173.2 2.9 %collective-permute-start.3 = (f32[2,128]{1,0:T(2,128)S(1)}, f32[2,128]{1,0:T(2,128)S(1)}, u32[]{:S(2)}, u32[]{:S(2)}) collective-permute-start(f32[2,128]{1,0:T(2,128)S(1)} %add.18), channel_id=1, source_target_pairs={{0,4},{1,5},{2,6},{3,7},{4,0},{5,1},{6,2},{7,3},{8,12},{9,13},{10,... | collective-permute-start | bytes 3080 | tf_op jit(solution)/shard_map/ppermute | solution.py:162
  176.1 1.4 collective-permute-done.3
  177.5 0.6 add.19
  178.1 2.4 %unpack.2 = (bf16[2,2,64,2048]{3,2,1,0:T(8,128)(2,1)}, bf16[2,2,64,2048]{3,2,1,0:T(8,128)(2,1)}, bf16[2,2,64,2048]{3,2,1,0:T(8,128)(2,1)}) custom-call(bf16[16,3,2,64,128]{4,3,2,1,0:T(8,128)(2,1)} %all-to-all-done.3.in_ref), custom_call_target="tpu_custom_call" | custom-call | tf_op jit(solution)/shard_map/unpack/pallas_call | solution.py:52
  180.5 22.2 %all-to-all-done.1.in_ref = bf16[16,3,2,64,128]{4,3,2,1,0:T(8,128)(2,1)} async-done(((bf16[16,3,2,64,128]{4,3,2,1,0:T(8,128)(2,1)}), bf16[16,3,2,64,128]{4,3,2,1,0:T(8,128)(2,1)}, u32[]{:S(2)}, u32[]{:S(2)}) %all-to-all-start.1) | async-done | bytes 1572896 | tf_op jit(solution)/shard_map/all_to_all | solution.py:176
  202.7 2.4 %unpack.3 = (bf16[2,2,64,2048]{3,2,1,0:T(8,128)(2,1)}, bf16[2,2,64,2048]{3,2,1,0:T(8,128)(2,1)}, bf16[2,2,64,2048]{3,2,1,0:T(8,128)(2,1)}) custom-call(bf16[16,3,2,64,128]{4,3,2,1,0:T(8,128)(2,1)} %all-to-all-done.1.in_ref, bf16[2,2,64,2048]{3,2,1,0:T(8,128)(2,1)} %get-tuple-element.16.refs_0_, ...), custom_call_target="tpu_custom_call", output_to_operand_aliasing={{0}: (1, {}), {1}: (2, {}), {2}: (3, {})} | custom-call | tf_op jit(solution)/shard_map/unpack/pallas_call | solution.py:52
  (6 shorter events, 0.0 us)
Async XLA Ops:
  3.4 59.0 %all-to-all-start.2 = ((bf16[16,4,2,64,128]{4,3,2,1,0:T(8,128)(2,1)}), bf16[16,4,2,64,128]{4,3,2,1,0:T(8,128)(2,1)}, u32[]{:S(2)}, u32[]{:S(2)}) async-start(bf16[16,4,2,64,128]{4,3,2,1,0:T(8,128)(2,1)} %pack.3), calls=%async_computation.2 | async-start | bytes 4194304 | tf_op jit(solution)/shard_map/all_to_all | solution.py:172
  62.4 54.0 %all-to-all-start = ((bf16[16,4,2,64,128]{4,3,2,1,0:T(8,128)(2,1)}), bf16[16,4,2,64,128]{4,3,2,1,0:T(8,128)(2,1)}, u32[]{:S(2)}, u32[]{:S(2)}) async-start(bf16[16,4,2,64,128]{4,3,2,1,0:T(8,128)(2,1)} %pack.2), calls=%async_computation | async-start | bytes 4194304 | tf_op jit(solution)/shard_map/all_to_all | solution.py:172
  116.4 43.5 %all-to-all-start.3 = ((bf16[16,3,2,64,128]{4,3,2,1,0:T(8,128)(2,1)}), bf16[16,3,2,64,128]{4,3,2,1,0:T(8,128)(2,1)}, u32[]{:S(2)}, u32[]{:S(2)}) async-start(bf16[16,3,2,64,128]{4,3,2,1,0:T(8,128)(2,1)} %get-tuple-element.15), calls=%async_computation.3 | async-start | bytes 3145728 | tf_op jit(solution)/shard_map/all_to_all | solution.py:176
  133.6 30.7 %copy-start = (f32[2,2,128]{2,1,0:T(2,128)S(1)}, f32[2,2,128]{2,1,0:T(2,128)}, u32[]{:S(2)}) copy-start(f32[2,2,128]{2,1,0:T(2,128)} %get-tuple-element.22) | copy-start | bytes 6148
  133.6 30.7 %copy-start.1 = (f32[2,2,128]{2,1,0:T(2,128)S(1)}, f32[2,2,128]{2,1,0:T(2,128)}, u32[]{:S(2)}) copy-start(f32[2,2,128]{2,1,0:T(2,128)} %get-tuple-element.23) | copy-start | bytes 6148
  159.9 42.8 %all-to-all-start.1 = ((bf16[16,3,2,64,128]{4,3,2,1,0:T(8,128)(2,1)}), bf16[16,3,2,64,128]{4,3,2,1,0:T(8,128)(2,1)}, u32[]{:S(2)}, u32[]{:S(2)}) async-start(bf16[16,3,2,64,128]{4,3,2,1,0:T(8,128)(2,1)} %get-tuple-element.14), calls=%async_computation.1 | async-start | bytes 3145728 | tf_op jit(solution)/shard_map/all_to_all | solution.py:176
  164.3 2.5 %collective-permute-start = (f32[2,128]{1,0:T(2,128)S(1)}, f32[2,128]{1,0:T(2,128)S(1)}, u32[]{:S(2)}, u32[]{:S(2)}) collective-permute-start(f32[2,128]{1,0:T(2,128)S(1)} %add.15), channel_id=1, source_target_pairs={{0,128},{128,0},{1,129},{129,1},{2,130},{130,2},{3,131},{131,3},{4... | collective-permute-start | bytes 3080 | tf_op jit(solution)/shard_map/ppermute | solution.py:162
  166.9 2.4 %collective-permute-start.1 = (f32[2,128]{1,0:T(2,128)S(1)}, f32[2,128]{1,0:T(2,128)S(1)}, u32[]{:S(2)}, u32[]{:S(2)}) collective-permute-start(f32[2,128]{1,0:T(2,128)S(1)} %add.16), channel_id=1, source_target_pairs={{0,1},{1,0},{2,3},{3,2},{4,5},{5,4},{6,7},{7,6},{8,9},{9,8},{10,11... | collective-permute-start | bytes 3080 | tf_op jit(solution)/shard_map/ppermute | solution.py:162
  169.3 3.9 %collective-permute-start.2 = (f32[2,128]{1,0:T(2,128)S(1)}, f32[2,128]{1,0:T(2,128)S(1)}, u32[]{:S(2)}, u32[]{:S(2)}) collective-permute-start(f32[2,128]{1,0:T(2,128)S(1)} %add.17), channel_id=1, source_target_pairs={{0,2},{1,3},{2,0},{3,1},{4,6},{5,7},{6,4},{7,5},{8,10},{9,11},{10,... | collective-permute-start | bytes 3080 | tf_op jit(solution)/shard_map/ppermute | solution.py:162
  173.2 4.3 %collective-permute-start.3 = (f32[2,128]{1,0:T(2,128)S(1)}, f32[2,128]{1,0:T(2,128)S(1)}, u32[]{:S(2)}, u32[]{:S(2)}) collective-permute-start(f32[2,128]{1,0:T(2,128)S(1)} %add.18), channel_id=1, source_target_pairs={{0,4},{1,5},{2,6},{3,7},{4,0},{5,1},{6,2},{7,3},{8,12},{9,13},{10,... | collective-permute-start | bytes 3080 | tf_op jit(solution)/shard_map/ppermute | solution.py:162

commit v3 on v2

--- a/solution.py
+++ b/solution.py
@@ -1,4 +1,3 @@
-import functools
 import math
 
 import jax
@@ -13,9 +12,24 @@
 DEPTH = 128
 BLOCK = 256
 VMEM_LIMIT = 63 * 1024 * 1024
-CHUNKS = ((0, 1), (1, 2))
+WINDOW = 4
+CHIPS = HEADS // 2
+ORDER = (1, 7, 2, 6, 3, 5, 4)
 F32 = jnp.float32
 BF16 = jnp.bfloat16
+
+
+def partner(index, slot):
+    z, core = index // 2, index % 2
+    return (z + (slot if core == 0 else CHIPS - slot)) % CHIPS * 2 + core
+
+
+def chip_of(index, slot):
+    return ((index >> 1) + jnp.where((index & 1) == 0, slot, CHIPS - slot)) & (CHIPS - 1)
+
+
+def source_of(index, slot):
+    return chip_of(index, CHIPS - slot)
 
 
 def pack_kernel(q_ref, k_ref, v_ref, g_ref, out_ref):
@@ -39,13 +53,36 @@
     )(*arrays)
 
 
+def compose(index, own, other):
+    _, kinds, items, rows, _ = own.shape
+
+    def kernel(index_ref, own_ref, other_ref, *messages):
+        for s in range(CHIPS):
+            chip = chip_of(index_ref[0], s)
+            messages[s][0] = own_ref[chip]
+            messages[s][1] = other_ref[chip]
+
+    return pl.pallas_call(
+        kernel,
+        grid_spec=pltpu.PrefetchScalarGridSpec(
+            num_scalar_prefetch=1,
+            grid=(items,),
+            in_specs=[pl.BlockSpec((CHIPS, kinds, 1, rows, DEPTH), lambda i, _: (0, 0, i, 0, 0))] * 2,
+            out_specs=[pl.BlockSpec((2, kinds, 1, rows, DEPTH), lambda i, _: (0, 0, i, 0, 0))] * CHIPS,
+        ),
+        out_shape=[jax.ShapeDtypeStruct((2, kinds, items, rows, DEPTH), BF16)] * CHIPS,
+        compiler_params=pltpu.CompilerParams(vmem_limit_bytes=VMEM_LIMIT),
+        name="compose",
+    )(index, own, other)
+
+
 def unpack_kernel(in_ref, *refs):
     for a, ref in enumerate(refs[-3:]):
         for h in range(HEADS):
             ref[0, 0, :, h * DEPTH : (h + 1) * DEPTH] = in_ref[h, a, 0]
 
 
-def unpack(arrived, first, clips, shape, earlier):
+def unpack_whole(arrived, first, clips, shape, earlier):
     _, frames, rows, width = shape
     items = clips * frames
     spec = pl.BlockSpec((1, 1, rows, width), lambda i: (first + i // frames, i % frames, 0, 0))
@@ -58,8 +95,36 @@
         out_shape=[jax.ShapeDtypeStruct(shape, BF16)] * 3,
         input_output_aliases={1 + i: i for i in range(len(earlier))},
         compiler_params=pltpu.CompilerParams(vmem_limit_bytes=VMEM_LIMIT),
+        name="unpack_whole",
+    )(arrived, *earlier)
+
+
+def unpack(index, messages, clip, shape, earlier):
+    _, frames, rows, width = shape
+
+    def kernel(index_ref, *refs):
+        for s in range(CHIPS):
+            chip = source_of(index_ref[0], s)
+            for hh in range(2):
+                head = 2 * chip + ((index_ref[0] & 1) ^ hh)
+                at = pl.ds(pl.multiple_of(head * DEPTH, DEPTH), DEPTH)
+                for a in range(3):
+                    refs[-3 + a][0, 0, :, at] = refs[s][hh, a, 0]
+
+    return pl.pallas_call(
+        kernel,
+        grid_spec=pltpu.PrefetchScalarGridSpec(
+            num_scalar_prefetch=1,
+            grid=(frames,),
+            in_specs=[pl.BlockSpec((2, 3, 1, rows, DEPTH), lambda i, _: (0, 0, i, 0, 0))] * CHIPS
+            + [pl.BlockSpec(memory_space=pl.ANY)] * len(earlier),
+            out_specs=[pl.BlockSpec((1, 1, rows, width), lambda i, _: (clip, i, 0, 0))] * 3,
+        ),
+        out_shape=[jax.ShapeDtypeStruct(shape, BF16)] * 3,
+        input_output_aliases={1 + CHIPS + i: i for i in range(len(earlier))},
+        compiler_params=pltpu.CompilerParams(vmem_limit_bytes=VMEM_LIMIT),
         name="unpack",
-    )(arrived, *earlier)
+    )(index, *messages, *earlier)
 
 
 def normalize(raw, gain):
@@ -79,15 +144,27 @@
     return lax.dot_general(a, b, (dims, ((), ())), preferred_element_type=F32)
 
 
-def attend_kernel(in_ref, gain_q_ref, gain_k_ref, out_ref, gains_ref, gv_ref, gk_ref):
+def attend_kernel(index_ref, in_ref, gain_q_ref, gain_k_ref, *refs):
+    *outs, gains_ref, gv_ref, gk_ref = refs
     sources, _, _, rows, depth = in_ref.shape
     total = sources * rows
     inverse = 1.0 / math.sqrt(depth)
     gain_q = gain_q_ref[...]
     gain_k = gain_k_ref[...]
 
+    low = (index_ref[0] & 1) == 0
+
     def whole(a):
         return in_ref[:, a, 0].reshape(total, depth)
+
+    def put(first, a, value):
+        value = value.reshape(-1, 2, rows, depth)
+        chips = pl.ds(first, value.shape[0])
+        if len(outs) == 1:
+            outs[0][chips, :, a, 0] = value
+        else:
+            outs[0][chips, a, 0] = jnp.where(low, value[:, 0], value[:, 1])
+            outs[1][chips, a, 0] = jnp.where(low, value[:, 1], value[:, 0])
 
     k_unit, k_scale, k_norm = normalize(whole(1), gain_k)
     values = whole(2)
@@ -115,36 +192,40 @@
             gk_ref[...] += grad_k
         grad_qn = dot(k_turned, dscore, ((1,), (0,))).T * inverse
         grad_q, term = restore(grad_qn, q_unit, q_scale, gain_q)
-        out_ref[part, 0, 0] = grad_q.reshape(each, rows, depth)
+        put(b * each // 2, 0, grad_q)
         term_q += jnp.sum(term, axis=0, keepdims=True)
     grad_k, term = restore(gk_ref[...] * inverse, k_unit, k_scale, gain_k)
-    out_ref[:, 1, 0] = grad_k.reshape(sources, rows, depth)
-    out_ref[:, 2, 0] = gv_ref[...].astype(BF16).reshape(sources, rows, depth)
+    put(0, 1, grad_k)
+    put(0, 2, gv_ref[...].astype(BF16))
     gains_ref[0, 0:1] = term_q
     gains_ref[0, 1:2] = jnp.sum(term, axis=0, keepdims=True)
 
 
-def attend(arrived, gain_q, gain_k):
+def attend(index, arrived, gain_q, gain_k, apart):
     sources, _, items, rows, depth = arrived.shape
     total = sources * rows
-    gain = pl.BlockSpec((1, depth), lambda i: (0, 0))
+    gain = pl.BlockSpec((1, depth), lambda i, _: (0, 0))
+    if apart:
+        outs = [(CHIPS, 3, items, rows, depth)] * 2
+        specs = [pl.BlockSpec((CHIPS, 3, 1, rows, depth), lambda i, _: (0, 0, i, 0, 0))] * 2
+    else:
+        outs = [(CHIPS, 2, 3, items, rows, depth)]
+        specs = [pl.BlockSpec((CHIPS, 2, 3, 1, rows, depth), lambda i, _: (0, 0, 0, i, 0, 0))]
     return pl.pallas_call(
         attend_kernel,
-        grid=(items,),
-        in_specs=[
-            pl.BlockSpec((sources, 4, 1, rows, depth), lambda i: (0, 0, i, 0, 0)),
-            gain,
-            gain,
-        ],
-        out_specs=[
-            pl.BlockSpec((sources, 3, 1, rows, depth), lambda i: (0, 0, i, 0, 0)),
-            pl.BlockSpec((1, 2, depth), lambda i: (i, 0, 0)),
-        ],
-        out_shape=[
-            jax.ShapeDtypeStruct((sources, 3, items, rows, depth), BF16),
-            jax.ShapeDtypeStruct((items, 2, depth), F32),
-        ],
-        scratch_shapes=[pltpu.VMEM((total, depth), F32)] * 2,
+        grid_spec=pltpu.PrefetchScalarGridSpec(
+            num_scalar_prefetch=1,
+            grid=(items,),
+            in_specs=[
+                pl.BlockSpec((sources, 4, 1, rows, depth), lambda i, _: (0, 0, i, 0, 0)),
+                gain,
+                gain,
+            ],
+            out_specs=specs + [pl.BlockSpec((1, 2, depth), lambda i, _: (i, 0, 0))],
+            scratch_shapes=[pltpu.VMEM((total, depth), F32)] * 2,
+        ),
+        out_shape=[jax.ShapeDtypeStruct(shape, BF16) for shape in outs]
+        + [jax.ShapeDtypeStruct((items, 2, depth), F32)],
         compiler_params=pltpu.CompilerParams(vmem_limit_bytes=VMEM_LIMIT),
         cost_estimate=pl.CostEstimate(
             flops=items * 10 * total * total * depth,
@@ -152,31 +233,54 @@
             transcendentals=items * total * total,
         ),
         name="attend",
-    )(arrived, gain_q, gain_k)
-
-
-def total_of(x):
+    )(index, arrived, gain_q, gain_k)
+
+
+def totals_of(x):
+    steps = []
     for axis in ("clip", "frame"):
         size, step = lax.axis_size(axis), 1
         while step < size:
             x = x + lax.ppermute(x, axis, [(i, i ^ step) for i in range(size)])
+            steps.append(x)
             step *= 2
-    return x
+    return steps
+
+
+def after(x, *earlier):
+    return lax.optimization_barrier((x, *earlier))[0] if earlier else x
+
+
+def swap(x):
+    return lax.ppermute(x, "patch", [(i, i ^ 1) for i in range(HEADS)])
+
+
+def exchange(x):
+    return lax.all_to_all(x, "patch", split_axis=0, concat_axis=0, tiled=True)
+
+
+def send(messages, earlier):
+    landed = list(messages)
+    for i, slot in enumerate(ORDER):
+        before = (landed[ORDER[i - WINDOW]],) if i >= WINDOW else (earlier,)
+        pairs = [(j, partner(j, slot)) for j in range(HEADS)]
+        landed[slot] = lax.ppermute(after(messages[slot], *before), "patch", pairs)
+    return landed
 
 
 def body(queries, keys, values, grad_out, gain_q, gain_k):
     arrays = (queries, keys, values, grad_out)
-    exchange = functools.partial(
-        lax.all_to_all, axis_name="patch", split_axis=0, concat_axis=0, tiled=True
-    )
-    arrived = [exchange(pack(arrays, first, last - first)) for first, last in CHUNKS]
-    done = [attend(a, gain_q, gain_k) for a in arrived]
-    grads = ()
-    for (first, last), (leaving, _) in zip(CHUNKS, done):
-        grads = unpack(exchange(leaving), first, last - first, queries.shape, grads)
-    terms = sum(jnp.sum(gains, axis=0) for _, gains in done)
-    gain_grads = total_of(terms).reshape(2, 1, DEPTH)
-    return (*grads, gain_grads)
+    shape = queries.shape
+    index = lax.axis_index("patch").reshape(1)
+    first, second = (exchange(pack(arrays, c, 1)) for c in range(2))
+    leaving, terms = attend(index, first, gain_q, gain_k, False)
+    first = exchange(leaving.reshape(HEADS, *leaving.shape[2:]))
+    own, other, more = attend(index, second, gain_q, gain_k, True)
+    gain_grads = totals_of(jnp.sum(terms + more, axis=0))[-1]
+    second = send(compose(index, own, swap(other)), gain_grads)
+    grads = unpack_whole(first, 0, 1, shape, ())
+    grads = unpack(index, second, 1, shape, grads)
+    return (*grads, gain_grads.reshape(2, 1, DEPTH))
 
 
 def solution(mesh):

time: 206 us -> 199 us (0.966)
  the two profiles are of different devices: /device:TPU:1 before, /device:TPU:32 now
where the time goes in v3:
time: 199 us; the launch traced here: 198 us
  waiting for transfers between devices  99.3 us (50%)
  starting transfers between devices  58.7 us (29%)
  Pallas kernels  37.1 us (19%)
    all_to_all x3, waiting for transfers between devices, exchange(): return lax.all_to_all(x, 'patch', split_axis=0, concat_axis=0, tiled=True)  80.1 us
    ppermute x7, starting transfers between devices, send(): landed[slot] = lax.ppermute(after(messages[slot], *before), 'patch', pairs)  27.6 us
    pallas_call x2, Pallas kernels, attend(): pl.pallas_call(attend_kernel, grid_spec=pltpu.PrefetchScalarGridSpec(num_...  24.3 us
    all_to_all x3, starting transfers between devices, exchange(): return lax.all_to_all(x, 'patch', split_axis=0, concat_axis=0, tiled=True)  21.7 us
    ppermute x7, waiting for transfers between devices, send(): landed[slot] = lax.ppermute(after(messages[slot], *before), 'patch', pairs)  11.3 us
    ppermute x4, starting transfers between devices, totals_of(): x = x + lax.ppermute(x, axis, [(i, i ^ step) for i in range(size)])  9.3 us
    ppermute x4, waiting for transfers between devices, totals_of(): x = x + lax.ppermute(x, axis, [(i, i ^ step) for i in range(size)])  7.99 us
    pallas_call x2, Pallas kernels, pack(): pl.pallas_call(pack_kernel, grid=(items,), in_specs=[spec] * 4, out_specs...  5.46 us
  transfers between devices with their start and end apart: 15, of which 11 were waited for; matrix products, arithmetic and copies ran while one was open for 1% of the time, Pallas kernels for 16%

profile of v3, /device:TPU:32, one launch (start us, length us, event | category | flops | bytes accessed | tf_op | source)
XLA Modules:
  0.0 198.1 jit_solution(7541831089159911903)
XLA Ops:
  0.6 2.7 %pack.3 = bf16[16,4,2,64,128]{4,3,2,1,0:T(8,128)(2,1)} custom-call(bf16[2,2,64,2048]{3,2,1,0:T(8,128)(2,1)} %q_ref.3, bf16[2,2,64,2048]{3,2,1,0:T(8,128)(2,1)} %k_ref.3, bf16[2,2,64,2048]{3,2,1,0:T(8,128)(2,1)} %v_ref.3, bf16[2,2,64,2048]{3,2,1,0:T(8,128)(2,1)} %g_ref.3), custom_call_target="tpu_custom_call" | custom-call | tf_op jit(solution)/shard_map/pack/pallas_call | solution.py:45
  3.4 8.6 %all-to-all-start.1 = ((bf16[16,4,2,64,128]{4,3,2,1,0:T(8,128)(2,1)}), bf16[16,4,2,64,128]{4,3,2,1,0:T(8,128)(2,1)}, u32[]{:S(2)}, u32[]{:S(2)}) async-start(bf16[16,4,2,64,128]{4,3,2,1,0:T(8,128)(2,1)} %pack.3), calls=%async_computation.1 | async-start | bytes 4194304 | tf_op jit(solution)/shard_map/all_to_all | solution.py:259
  11.9 2.7 %pack.2 = bf16[16,4,2,64,128]{4,3,2,1,0:T(8,128)(2,1)} custom-call(bf16[2,2,64,2048]{3,2,1,0:T(8,128)(2,1)} %q_ref.3, bf16[2,2,64,2048]{3,2,1,0:T(8,128)(2,1)} %k_ref.3, bf16[2,2,64,2048]{3,2,1,0:T(8,128)(2,1)} %v_ref.3, bf16[2,2,64,2048]{3,2,1,0:T(8,128)(2,1)} %g_ref.3), custom_call_target="tpu_custom_call" | custom-call | tf_op jit(solution)/shard_map/pack/pallas_call | solution.py:45
  14.7 44.8 %all-to-all-done.1.in_ref = bf16[16,4,2,64,128]{4,3,2,1,0:T(8,128)(2,1)} async-done(((bf16[16,4,2,64,128]{4,3,2,1,0:T(8,128)(2,1)}), bf16[16,4,2,64,128]{4,3,2,1,0:T(8,128)(2,1)}, u32[]{:S(2)}, u32[]{:S(2)}) %all-to-all-start.1) | async-done | bytes 2097184 | tf_op jit(solution)/shard_map/all_to_all | solution.py:259
  59.4 6.5 %all-to-all-start = ((bf16[16,4,2,64,128]{4,3,2,1,0:T(8,128)(2,1)}), bf16[16,4,2,64,128]{4,3,2,1,0:T(8,128)(2,1)}, u32[]{:S(2)}, u32[]{:S(2)}) async-start(bf16[16,4,2,64,128]{4,3,2,1,0:T(8,128)(2,1)} %pack.2), calls=%async_computation | async-start | bytes 4194304 | tf_op jit(solution)/shard_map/all_to_all | solution.py:259
  66.0 12.2 %attend.3 = (bf16[8,2,3,2,64,128]{5,4,3,2,1,0:T(8,128)(2,1)}, f32[2,2,128]{2,1,0:T(2,128)}) custom-call(s32[1]{0:T(128)} %bitcast.index_ref, bf16[16,4,2,64,128]{4,3,2,1,0:T(8,128)(2,1)} %all-to-all-done.1.in_ref, f32[1,128]{1,0:T(1,128)} %gain_q_ref.3, f32[1,128]{1,0:T(1,128)} %gain_k_ref.3), custom_call_target="tpu_custom_call" | custom-call | flops 2684354560 | bytes 3670016 | tf_op jit(solution)/shard_map/attend/pallas_call | solution.py:214
  78.2 35.3 %all-to-all-done.in_ref = bf16[16,4,2,64,128]{4,3,2,1,0:T(8,128)(2,1)} async-done(((bf16[16,4,2,64,128]{4,3,2,1,0:T(8,128)(2,1)}), bf16[16,4,2,64,128]{4,3,2,1,0:T(8,128)(2,1)}, u32[]{:S(2)}, u32[]{:S(2)}) %all-to-all-start) | async-done | bytes 2097184 | tf_op jit(solution)/shard_map/all_to_all | solution.py:259
  113.5 6.5 %all-to-all-start.2 = ((bf16[16,3,2,64,128]{4,3,2,1,0:T(8,128)(2,1)}), bf16[16,3,2,64,128]{4,3,2,1,0:T(8,128)(2,1)}, u32[]{:S(2)}, u32[]{:S(2)}) async-start(bf16[16,3,2,64,128]{4,3,2,1,0:T(8,128)(2,1)} %bitcast.3), calls=%async_computation.2 | async-start | bytes 3145728 | tf_op jit(solution)/shard_map/all_to_all | solution.py:259
  120.0 0.0 copy-start.6
  120.0 12.2 %attend.2 = (bf16[8,3,2,64,128]{4,3,2,1,0:T(8,128)(2,1)}, bf16[8,3,2,64,128]{4,3,2,1,0:T(8,128)(2,1)}, f32[2,2,128]{2,1,0:T(2,128)}) custom-call(s32[1]{0:T(128)} %bitcast.index_ref, bf16[16,4,2,64,128]{4,3,2,1,0:T(8,128)(2,1)} %all-to-all-done.in_ref, f32[1,128]{1,0:T(1,128)} %gain_q_ref.3, f32[1,128]{1,0:T(1,128)} %gain_k_ref.3), custom_call_target="tpu_custom_call" | custom-call | flops 2684354560 | bytes 3670016 | tf_op jit(solution)/shard_map/attend/pallas_call | solution.py:214
  132.2 0.1 collective-permute-start
  132.3 0.0 copy-done.6
  132.3 0.7 add_reduce_fusion
  133.0 1.6 collective-permute-start.1
  134.6 2.0 %collective-permute-done.1 = f32[2,128]{1,0:T(2,128)S(1)} collective-permute-done((f32[2,128]{1,0:T(2,128)S(1)}, f32[2,128]{1,0:T(2,128)S(1)}, u32[]{:S(2)}, u32[]{:S(2)}) %collective-permute-start.1) | collective-permute-done | bytes 1056 | tf_op jit(solution)/shard_map/ppermute | solution.py:244
  136.6 1.5 collective-permute-start.2
  138.1 2.1 %collective-permute-done.2 = f32[2,128]{1,0:T(2,128)S(1)} collective-permute-done((f32[2,128]{1,0:T(2,128)S(1)}, f32[2,128]{1,0:T(2,128)S(1)}, u32[]{:S(2)}, u32[]{:S(2)}) %collective-permute-start.2) | collective-permute-done | bytes 1056 | tf_op jit(solution)/shard_map/ppermute | solution.py:244
  140.2 3.0 %collective-permute-start.3 = (f32[2,128]{1,0:T(2,128)S(1)}, f32[2,128]{1,0:T(2,128)S(1)}, u32[]{:S(2)}, u32[]{:S(2)}) collective-permute-start(f32[2,128]{1,0:T(2,128)S(1)} %add.17), channel_id=1, source_target_pairs={{0,2},{1,3},{2,0},{3,1},{4,6},{5,7},{6,4},{7,5},{8,10},{9,11},{10,... | collective-permute-start | bytes 3080 | tf_op jit(solution)/shard_map/ppermute | solution.py:244
  143.2 2.0 %collective-permute-done.3 = f32[2,128]{1,0:T(2,128)S(1)} collective-permute-done((f32[2,128]{1,0:T(2,128)S(1)}, f32[2,128]{1,0:T(2,128)S(1)}, u32[]{:S(2)}, u32[]{:S(2)}) %collective-permute-start.3) | collective-permute-done | bytes 1056 | tf_op jit(solution)/shard_map/ppermute | solution.py:244
  145.3 3.2 %collective-permute-start.4 = (f32[2,128]{1,0:T(2,128)S(1)}, f32[2,128]{1,0:T(2,128)S(1)}, u32[]{:S(2)}, u32[]{:S(2)}) collective-permute-start(f32[2,128]{1,0:T(2,128)S(1)} %add.18), channel_id=1, source_target_pairs={{0,4},{1,5},{2,6},{3,7},{4,0},{5,1},{6,2},{7,3},{8,12},{9,13},{10,... | collective-permute-start | bytes 3080 | tf_op jit(solution)/shard_map/ppermute | solution.py:244
  148.5 1.9 collective-permute-done.4
  150.4 0.6 add.19
  150.9 0.0 collective-permute-done.other_ref
  150.9 0.0 copy-start
  150.9 0.9 copy-done
  151.8 2.3 %compose.1 = (bf16[2,3,2,64,128]{4,3,2,1,0:T(8,128)(2,1)}, bf16[2,3,2,64,128]{4,3,2,1,0:T(8,128)(2,1)}, bf16[2,3,2,64,128]{4,3,2,1,0:T(8,128)(2,1)}, bf16[2,3,2,...) custom-call(s32[1]{0:T(128)} %bitcast.index_ref, ...), custom_call_target="tpu_custom_call" | custom-call | tf_op jit(solution)/shard_map/compose/pallas_call | solution.py:65
  154.1 0.4 collective-permute-start.9
  154.5 2.6 %collective-permute-start.6 = (bf16[2,3,2,64,128]{4,3,2,1,0:T(8,128)(2,1)}, bf16[2,3,2,64,128]{4,3,2,1,0:T(8,128)(2,1)S(1)}, u32[]{:S(2)}, u32[]{:S(2)}) collective-permute-start(bf16[2,3,2,64,128]{4,3,2,1,0:T(8,128)(2,1)} %get-tuple-element.38), channel_id=1, source_target_pairs={{0,32},{8,104},{16,48},{24,120},{32,64},{40,8},{48,80},{56,24},{64... | collective-permute-start | bytes 589832 | tf_op jit(solution)/shard_map/ppermute | solution.py:267
  157.1 2.7 %collective-permute-start.5 = (bf16[2,3,2,64,128]{4,3,2,1,0:T(8,128)(2,1)}, bf16[2,3,2,64,128]{4,3,2,1,0:T(8,128)(2,1)S(1)}, u32[]{:S(2)}, u32[]{:S(2)}) collective-permute-start(bf16[2,3,2,64,128]{4,3,2,1,0:T(8,128)(2,1)} %get-tuple-element.36), channel_id=1, source_target_pairs={{0,16},{8,120},{16,32},{24,8},{32,48},{40,24},{48,64},{56,40},{64,... | collective-permute-start | bytes 589832 | tf_op jit(solution)/shard_map/ppermute | solution.py:267
  159.8 0.6 collective-permute-start.11
  160.3 3.7 %collective-permute-done.9.refs_7_ = bf16[2,3,2,64,128]{4,3,2,1,0:T(8,128)(2,1)S(1)} collective-permute-done((bf16[2,3,2,64,128]{4,3,2,1,0:T(8,128)(2,1)}, bf16[2,3,2,64,128]{4,3,2,1,0:T(8,128)(2,1)S(1)}, u32[]{:S(2)}, u32[]{:S(2)}) %collective-permute-start.9) | collective-permute-done | bytes 196640 | tf_op jit(solution)/shard_map/ppermute | solution.py:267
  164.0 0.0 copy-start.1
  164.0 3.4 %collective-permute-start.10 = (bf16[2,3,2,64,128]{4,3,2,1,0:T(8,128)(2,1)}, bf16[2,3,2,64,128]{4,3,2,1,0:T(8,128)(2,1)S(1)}, u32[]{:S(2)}, u32[]{:S(2)}) collective-permute-start(bf16[2,3,2,64,128]{4,3,2,1,0:T(8,128)(2,1)} %get-tuple-element.46), channel_id=1, source_target_pairs={{0,80},{8,56},{16,96},{24,72},{32,112},{40,88},{48,0},{56,104},{64... | collective-permute-start | bytes 589832 | tf_op jit(solution)/shard_map/ppermute | solution.py:267
  167.4 1.6 collective-permute-done.6.refs_2_
  169.0 0.0 copy-start.2
  169.0 3.1 %collective-permute-start.8 = (bf16[2,3,2,64,128]{4,3,2,1,0:T(8,128)(2,1)}, bf16[2,3,2,64,128]{4,3,2,1,0:T(8,128)(2,1)}, u32[]{:S(2)}, u32[]{:S(2)}) collective-permute-start(bf16[2,3,2,64,128]{4,3,2,1,0:T(8,128)(2,1)} %get-tuple-element.42), channel_id=1, source_target_pairs={{0,64},{8,72},{16,80},{24,88},{32,96},{40,104},{48,112},{56,120},{... | collective-permute-start | bytes 589832 | tf_op jit(solution)/shard_map/ppermute | solution.py:267
  172.1 2.6 %collective-permute-done.5.refs_1_ = bf16[2,3,2,64,128]{4,3,2,1,0:T(8,128)(2,1)S(1)} collective-permute-done((bf16[2,3,2,64,128]{4,3,2,1,0:T(8,128)(2,1)}, bf16[2,3,2,64,128]{4,3,2,1,0:T(8,128)(2,1)S(1)}, u32[]{:S(2)}, u32[]{:S(2)}) %collective-permute-start.5) | collective-permute-done | bytes 196640 | tf_op jit(solution)/shard_map/ppermute | solution.py:267
  174.7 0.0 copy-start.3
  174.7 14.8 %collective-permute-start.7 = (bf16[2,3,2,64,128]{4,3,2,1,0:T(8,128)(2,1)}, bf16[2,3,2,64,128]{4,3,2,1,0:T(8,128)(2,1)}, u32[]{:S(2)}, u32[]{:S(2)}) collective-permute-start(bf16[2,3,2,64,128]{4,3,2,1,0:T(8,128)(2,1)} %get-tuple-element.40), channel_id=1, source_target_pairs={{0,48},{8,88},{16,64},{24,104},{32,80},{40,120},{48,96},{56,8},{64... | collective-permute-start | bytes 589832 | tf_op jit(solution)/shard_map/ppermute | solution.py:267
  189.6 0.0 all-to-all-done.2.in_ref
  189.6 2.4 %unpack_whole.1 = (bf16[2,2,64,2048]{3,2,1,0:T(8,128)(2,1)}, bf16[2,2,64,2048]{3,2,1,0:T(8,128)(2,1)}, bf16[2,2,64,2048]{3,2,1,0:T(8,128)(2,1)}) custom-call(bf16[16,3,2,64,128]{4,3,2,1,0:T(8,128)(2,1)} %all-to-all-done.2.in_ref), custom_call_target="tpu_custom_call" | custom-call | tf_op jit(solution)/shard_map/unpack_whole/pallas_call | solution.py:89
  192.0 0.0 collective-permute-done.11.refs_6_
  192.0 0.0 copy-start.4
  192.0 0.0 collective-permute-done.10.refs_5_
  192.0 0.0 copy-start.5
  192.0 2.2 %collective-permute-done.8.refs_4_ = bf16[2,3,2,64,128]{4,3,2,1,0:T(8,128)(2,1)} collective-permute-done((bf16[2,3,2,64,128]{4,3,2,1,0:T(8,128)(2,1)}, bf16[2,3,2,64,128]{4,3,2,1,0:T(8,128)(2,1)}, u32[]{:S(2)}, u32[]{:S(2)}) %collective-permute-start.8) | collective-permute-done | bytes 196640 | tf_op jit(solution)/shard_map/ppermute | solution.py:267
  194.2 1.2 collective-permute-done.7.refs_3_
  195.4 0.0 copy-done.1
  195.4 0.0 copy-done.2
  195.4 0.0 copy-done.3
  195.4 0.0 copy-done.4
  195.4 0.0 copy-done.5
  195.4 2.6 %unpack.1 = (bf16[2,2,64,2048]{3,2,1,0:T(8,128)(2,1)}, bf16[2,2,64,2048]{3,2,1,0:T(8,128)(2,1)}, bf16[2,2,64,2048]{3,2,1,0:T(8,128)(2,1)}) custom-call(s32[1]{0:T(128)} %bitcast.index_ref, bf16[2,3,2,64,128]{4,3,2,1,0:T(8,128)(2,1)} %get-tuple-element.32.refs_0_, ...), custom_call_target="tpu_custom_call", output_to_operand_aliasing={{0}: (9, {}), {1}: (10, {}), {2}: (11, {})} | custom-call | tf_op jit(solution)/shard_map/unpack/pallas_call | solution.py:114
  (3 shorter events, 0.0 us)
Async XLA Ops:
  3.4 56.1 %all-to-all-start.1 = ((bf16[16,4,2,64,128]{4,3,2,1,0:T(8,128)(2,1)}), bf16[16,4,2,64,128]{4,3,2,1,0:T(8,128)(2,1)}, u32[]{:S(2)}, u32[]{:S(2)}) async-start(bf16[16,4,2,64,128]{4,3,2,1,0:T(8,128)(2,1)} %pack.3), calls=%async_computation.1 | async-start | bytes 4194304 | tf_op jit(solution)/shard_map/all_to_all | solution.py:259
  59.4 54.0 %all-to-all-start = ((bf16[16,4,2,64,128]{4,3,2,1,0:T(8,128)(2,1)}), bf16[16,4,2,64,128]{4,3,2,1,0:T(8,128)(2,1)}, u32[]{:S(2)}, u32[]{:S(2)}) async-start(bf16[16,4,2,64,128]{4,3,2,1,0:T(8,128)(2,1)} %pack.2), calls=%async_computation | async-start | bytes 4194304 | tf_op jit(solution)/shard_map/all_to_all | solution.py:259
  113.5 76.1 %all-to-all-start.2 = ((bf16[16,3,2,64,128]{4,3,2,1,0:T(8,128)(2,1)}), bf16[16,3,2,64,128]{4,3,2,1,0:T(8,128)(2,1)}, u32[]{:S(2)}, u32[]{:S(2)}) async-start(bf16[16,3,2,64,128]{4,3,2,1,0:T(8,128)(2,1)} %bitcast.3), calls=%async_computation.2 | async-start | bytes 3145728 | tf_op jit(solution)/shard_map/all_to_all | solution.py:259
  120.0 12.3 %copy-start.6 = (f32[2,2,128]{2,1,0:T(2,128)S(1)}, f32[2,2,128]{2,1,0:T(2,128)}, u32[]{:S(2)}) copy-start(f32[2,2,128]{2,1,0:T(2,128)} %get-tuple-element.34) | copy-start | bytes 6148
  132.2 18.7 %collective-permute-start = (bf16[8,3,2,64,128]{4,3,2,1,0:T(8,128)(2,1)}, bf16[8,3,2,64,128]{4,3,2,1,0:T(8,128)(2,1)S(1)}, u32[]{:S(2)}, u32[]{:S(2)}) collective-permute-start(bf16[8,3,2,64,128]{4,3,2,1,0:T(8,128)(2,1)} %get-tuple-element.31), channel_id=1, source_target_pairs={{0,8},{8,0},{16,24},{24,16},{32,40},{40,32},{48,56},{56,48},{64,72... | collective-permute-start | bytes 2359304 | tf_op jit(solution)/shard_map/ppermute | solution.py:255
  133.0 3.6 %collective-permute-start.1 = (f32[2,128]{1,0:T(2,128)S(1)}, f32[2,128]{1,0:T(2,128)S(1)}, u32[]{:S(2)}, u32[]{:S(2)}) collective-permute-start(f32[2,128]{1,0:T(2,128)S(1)} %add_reduce_fusion), channel_id=1, source_target_pairs={{0,128},{128,0},{1,129},{129,1},{2,130},{130,2},{3,131},{131,3},{4... | collective-permute-start | bytes 3080 | tf_op jit(solution)/shard_map/ppermute | solution.py:244
  136.6 3.6 %collective-permute-start.2 = (f32[2,128]{1,0:T(2,128)S(1)}, f32[2,128]{1,0:T(2,128)S(1)}, u32[]{:S(2)}, u32[]{:S(2)}) collective-permute-start(f32[2,128]{1,0:T(2,128)S(1)} %add.16), channel_id=1, source_target_pairs={{0,1},{1,0},{2,3},{3,2},{4,5},{5,4},{6,7},{7,6},{8,9},{9,8},{10,11... | collective-permute-start | bytes 3080 | tf_op jit(solution)/shard_map/ppermute | solution.py:244
  140.2 5.1 %collective-permute-start.3 = (f32[2,128]{1,0:T(2,128)S(1)}, f32[2,128]{1,0:T(2,128)S(1)}, u32[]{:S(2)}, u32[]{:S(2)}) collective-permute-start(f32[2,128]{1,0:T(2,128)S(1)} %add.17), channel_id=1, source_target_pairs={{0,2},{1,3},{2,0},{3,1},{4,6},{5,7},{6,4},{7,5},{8,10},{9,11},{10,... | collective-permute-start | bytes 3080 | tf_op jit(solution)/shard_map/ppermute | solution.py:244
  145.3 5.1 %collective-permute-start.4 = (f32[2,128]{1,0:T(2,128)S(1)}, f32[2,128]{1,0:T(2,128)S(1)}, u32[]{:S(2)}, u32[]{:S(2)}) collective-permute-start(f32[2,128]{1,0:T(2,128)S(1)} %add.18), channel_id=1, source_target_pairs={{0,4},{1,5},{2,6},{3,7},{4,0},{5,1},{6,2},{7,3},{8,12},{9,13},{10,... | collective-permute-start | bytes 3080 | tf_op jit(solution)/shard_map/ppermute | solution.py:244
  150.9 0.9 copy-start
  154.1 9.9 %collective-permute-start.9 = (bf16[2,3,2,64,128]{4,3,2,1,0:T(8,128)(2,1)}, bf16[2,3,2,64,128]{4,3,2,1,0:T(8,128)(2,1)S(1)}, u32[]{:S(2)}, u32[]{:S(2)}) collective-permute-start(bf16[2,3,2,64,128]{4,3,2,1,0:T(8,128)(2,1)} %get-tuple-element.45), channel_id=1, source_target_pairs={{0,112},{8,24},{16,0},{24,40},{32,16},{40,56},{48,32},{56,72},{64,... | collective-permute-start | bytes 589832 | tf_op jit(solution)/shard_map/ppermute | solution.py:267
  154.5 14.5 %collective-permute-start.6 = (bf16[2,3,2,64,128]{4,3,2,1,0:T(8,128)(2,1)}, bf16[2,3,2,64,128]{4,3,2,1,0:T(8,128)(2,1)S(1)}, u32[]{:S(2)}, u32[]{:S(2)}) collective-permute-start(bf16[2,3,2,64,128]{4,3,2,1,0:T(8,128)(2,1)} %get-tuple-element.38), channel_id=1, source_target_pairs={{0,32},{8,104},{16,48},{24,120},{32,64},{40,8},{48,80},{56,24},{64... | collective-permute-start | bytes 589832 | tf_op jit(solution)/shard_map/ppermute | solution.py:267
  157.1 17.6 %collective-permute-start.5 = (bf16[2,3,2,64,128]{4,3,2,1,0:T(8,128)(2,1)}, bf16[2,3,2,64,128]{4,3,2,1,0:T(8,128)(2,1)S(1)}, u32[]{:S(2)}, u32[]{:S(2)}) collective-permute-start(bf16[2,3,2,64,128]{4,3,2,1,0:T(8,128)(2,1)} %get-tuple-element.36), channel_id=1, source_target_pairs={{0,16},{8,120},{16,32},{24,8},{32,48},{40,24},{48,64},{56,40},{64,... | collective-permute-start | bytes 589832 | tf_op jit(solution)/shard_map/ppermute | solution.py:267
  159.8 32.2 %collective-permute-start.11 = (bf16[2,3,2,64,128]{4,3,2,1,0:T(8,128)(2,1)}, bf16[2,3,2,64,128]{4,3,2,1,0:T(8,128)(2,1)S(1)}, u32[]{:S(2)}, u32[]{:S(2)}) collective-permute-start(bf16[2,3,2,64,128]{4,3,2,1,0:T(8,128)(2,1)} %get-tuple-element.48), channel_id=1, source_target_pairs={{0,96},{8,40},{16,112},{24,56},{32,0},{40,72},{48,16},{56,88},{64,... | collective-permute-start | bytes 589832 | tf_op jit(solution)/shard_map/ppermute | solution.py:267
  164.0 31.4 %copy-start.1 = (bf16[2,3,2,64,128]{4,3,2,1,0:T(8,128)(2,1)}, bf16[2,3,2,64,128]{4,3,2,1,0:T(8,128)(2,1)S(1)}, u32[]{:S(2)}) copy-start(bf16[2,3,2,64,128]{4,3,2,1,0:T(8,128)(2,1)S(1)} %collective-permute-done.9.refs_7_) | copy-start | bytes 589828
  164.0 28.0 %collective-permute-start.10 = (bf16[2,3,2,64,128]{4,3,2,1,0:T(8,128)(2,1)}, bf16[2,3,2,64,128]{4,3,2,1,0:T(8,128)(2,1)S(1)}, u32[]{:S(2)}, u32[]{:S(2)}) collective-permute-start(bf16[2,3,2,64,128]{4,3,2,1,0:T(8,128)(2,1)} %get-tuple-element.46), channel_id=1, source_target_pairs={{0,80},{8,56},{16,96},{24,72},{32,112},{40,88},{48,0},{56,104},{64... | collective-permute-start | bytes 589832 | tf_op jit(solution)/shard_map/ppermute | solution.py:267
  169.0 26.4 %copy-start.2 = (bf16[2,3,2,64,128]{4,3,2,1,0:T(8,128)(2,1)}, bf16[2,3,2,64,128]{4,3,2,1,0:T(8,128)(2,1)S(1)}, u32[]{:S(2)}) copy-start(bf16[2,3,2,64,128]{4,3,2,1,0:T(8,128)(2,1)S(1)} %collective-permute-done.6.refs_2_) | copy-start | bytes 589828
  169.0 25.2 %collective-permute-start.8 = (bf16[2,3,2,64,128]{4,3,2,1,0:T(8,128)(2,1)}, bf16[2,3,2,64,128]{4,3,2,1,0:T(8,128)(2,1)}, u32[]{:S(2)}, u32[]{:S(2)}) collective-permute-start(bf16[2,3,2,64,128]{4,3,2,1,0:T(8,128)(2,1)} %get-tuple-element.42), channel_id=1, source_target_pairs={{0,64},{8,72},{16,80},{24,88},{32,96},{40,104},{48,112},{56,120},{... | collective-permute-start | bytes 589832 | tf_op jit(solution)/shard_map/ppermute | solution.py:267
  174.7 20.7 %copy-start.3 = (bf16[2,3,2,64,128]{4,3,2,1,0:T(8,128)(2,1)}, bf16[2,3,2,64,128]{4,3,2,1,0:T(8,128)(2,1)S(1)}, u32[]{:S(2)}) copy-start(bf16[2,3,2,64,128]{4,3,2,1,0:T(8,128)(2,1)S(1)} %collective-permute-done.5.refs_1_) | copy-start | bytes 589828
  174.7 20.7 %collective-permute-start.7 = (bf16[2,3,2,64,128]{4,3,2,1,0:T(8,128)(2,1)}, bf16[2,3,2,64,128]{4,3,2,1,0:T(8,128)(2,1)}, u32[]{:S(2)}, u32[]{:S(2)}) collective-permute-start(bf16[2,3,2,64,128]{4,3,2,1,0:T(8,128)(2,1)} %get-tuple-element.40), channel_id=1, source_target_pairs={{0,48},{8,88},{16,64},{24,104},{32,80},{40,120},{48,96},{56,8},{64... | collective-permute-start | bytes 589832 | tf_op jit(solution)/shard_map/ppermute | solution.py:267
  192.0 3.4 %copy-start.4 = (bf16[2,3,2,64,128]{4,3,2,1,0:T(8,128)(2,1)}, bf16[2,3,2,64,128]{4,3,2,1,0:T(8,128)(2,1)S(1)}, u32[]{:S(2)}) copy-start(bf16[2,3,2,64,128]{4,3,2,1,0:T(8,128)(2,1)S(1)} %collective-permute-done.11.refs_6_) | copy-start | bytes 589828
  192.0 3.4 %copy-start.5 = (bf16[2,3,2,64,128]{4,3,2,1,0:T(8,128)(2,1)}, bf16[2,3,2,64,128]{4,3,2,1,0:T(8,128)(2,1)S(1)}, u32[]{:S(2)}) copy-start(bf16[2,3,2,64,128]{4,3,2,1,0:T(8,128)(2,1)S(1)} %collective-permute-done.10.refs_5_) | copy-start | bytes 589828

commit v4 on v3

--- a/solution.py
+++ b/solution.py
@@ -12,7 +12,7 @@
 DEPTH = 128
 BLOCK = 256
 VMEM_LIMIT = 63 * 1024 * 1024
-WINDOW = 4
+WINDOW = 5
 CHIPS = HEADS // 2
 ORDER = (1, 7, 2, 6, 3, 5, 4)
 F32 = jnp.float32

time: 199 us -> 197 us (0.990); the launches traced: 198 us -> 194 us
  starting transfers between devices: 58.7 us -> 45.8 us
  waiting for transfers between devices: 99.3 us -> 108 us
    ppermute x7, starting transfers between devices: 27.6 us -> 14.7 us  [send(): landed[slot] = lax.ppermute(after(messages[slot], *before), 'patch', pairs)]
    ppermute x7, waiting for transfers between devices: 11.3 us -> 20 us  [send(): landed[slot] = lax.ppermute(after(messages[slot], *before), 'patch', pairs)]
  transfers between devices with their start and end apart: 15 -> 15, of which waited for: 11 -> 10; matrix products, arithmetic and copies ran while one was open for 1% -> 1% of each run, Pallas kernels for 16% -> 16%
where the time goes in v4:
time: 197 us; the launch traced here: 194 us
  waiting for transfers between devices  108 us (55%)
  starting transfers between devices  45.8 us (23%)
  Pallas kernels  37.1 us (19%)
    all_to_all x3, waiting for transfers between devices, exchange(): return lax.all_to_all(x, 'patch', split_axis=0, concat_axis=0, tiled=True)  80.1 us
    pallas_call x2, Pallas kernels, attend(): pl.pallas_call(attend_kernel, grid_spec=pltpu.PrefetchScalarGridSpec(num_...  24.3 us
    all_to_all x3, starting transfers between devices, exchange(): return lax.all_to_all(x, 'patch', split_axis=0, concat_axis=0, tiled=True)  21.7 us
    ppermute x7, waiting for transfers between devices, send(): landed[slot] = lax.ppermute(after(messages[slot], *before), 'patch', pairs)  20 us
    ppermute x7, starting transfers between devices, send(): landed[slot] = lax.ppermute(after(messages[slot], *before), 'patch', pairs)  14.7 us
    ppermute x4, starting transfers between devices, totals_of(): x = x + lax.ppermute(x, axis, [(i, i ^ step) for i in range(size)])  9.3 us
    ppermute x4, waiting for transfers between devices, totals_of(): x = x + lax.ppermute(x, axis, [(i, i ^ step) for i in range(size)])  7.99 us
    pallas_call x2, Pallas kernels, pack(): pl.pallas_call(pack_kernel, grid=(items,), in_specs=[spec] * 4, out_specs...  5.46 us
  transfers between devices with their start and end apart: 15, of which 10 were waited for; matrix products, arithmetic and copies ran while one was open for 1% of the time, Pallas kernels for 16%

profile of v4, /device:TPU:32, one launch (start us, length us, event | category | flops | bytes accessed | tf_op | source)
XLA Modules:
  0.0 194.0 jit_solution(424279492615346203)
XLA Ops:
  0.6 2.7 %pack.3 = bf16[16,4,2,64,128]{4,3,2,1,0:T(8,128)(2,1)} custom-call(bf16[2,2,64,2048]{3,2,1,0:T(8,128)(2,1)} %q_ref.3, bf16[2,2,64,2048]{3,2,1,0:T(8,128)(2,1)} %k_ref.3, bf16[2,2,64,2048]{3,2,1,0:T(8,128)(2,1)} %v_ref.3, bf16[2,2,64,2048]{3,2,1,0:T(8,128)(2,1)} %g_ref.3), custom_call_target="tpu_custom_call" | custom-call | tf_op jit(solution)/shard_map/pack/pallas_call | solution.py:45
  3.4 8.6 %all-to-all-start.1 = ((bf16[16,4,2,64,128]{4,3,2,1,0:T(8,128)(2,1)}), bf16[16,4,2,64,128]{4,3,2,1,0:T(8,128)(2,1)}, u32[]{:S(2)}, u32[]{:S(2)}) async-start(bf16[16,4,2,64,128]{4,3,2,1,0:T(8,128)(2,1)} %pack.3), calls=%async_computation.1 | async-start | bytes 4194304 | tf_op jit(solution)/shard_map/all_to_all | solution.py:259
  11.9 2.7 %pack.2 = bf16[16,4,2,64,128]{4,3,2,1,0:T(8,128)(2,1)} custom-call(bf16[2,2,64,2048]{3,2,1,0:T(8,128)(2,1)} %q_ref.3, bf16[2,2,64,2048]{3,2,1,0:T(8,128)(2,1)} %k_ref.3, bf16[2,2,64,2048]{3,2,1,0:T(8,128)(2,1)} %v_ref.3, bf16[2,2,64,2048]{3,2,1,0:T(8,128)(2,1)} %g_ref.3), custom_call_target="tpu_custom_call" | custom-call | tf_op jit(solution)/shard_map/pack/pallas_call | solution.py:45
  14.7 44.8 %all-to-all-done.1.in_ref = bf16[16,4,2,64,128]{4,3,2,1,0:T(8,128)(2,1)} async-done(((bf16[16,4,2,64,128]{4,3,2,1,0:T(8,128)(2,1)}), bf16[16,4,2,64,128]{4,3,2,1,0:T(8,128)(2,1)}, u32[]{:S(2)}, u32[]{:S(2)}) %all-to-all-start.1) | async-done | bytes 2097184 | tf_op jit(solution)/shard_map/all_to_all | solution.py:259
  59.4 6.5 %all-to-all-start = ((bf16[16,4,2,64,128]{4,3,2,1,0:T(8,128)(2,1)}), bf16[16,4,2,64,128]{4,3,2,1,0:T(8,128)(2,1)}, u32[]{:S(2)}, u32[]{:S(2)}) async-start(bf16[16,4,2,64,128]{4,3,2,1,0:T(8,128)(2,1)} %pack.2), calls=%async_computation | async-start | bytes 4194304 | tf_op jit(solution)/shard_map/all_to_all | solution.py:259
  66.0 12.2 %attend.3 = (bf16[8,2,3,2,64,128]{5,4,3,2,1,0:T(8,128)(2,1)}, f32[2,2,128]{2,1,0:T(2,128)}) custom-call(s32[1]{0:T(128)} %bitcast.index_ref, bf16[16,4,2,64,128]{4,3,2,1,0:T(8,128)(2,1)} %all-to-all-done.1.in_ref, f32[1,128]{1,0:T(1,128)} %gain_q_ref.3, f32[1,128]{1,0:T(1,128)} %gain_k_ref.3), custom_call_target="tpu_custom_call" | custom-call | flops 2684354560 | bytes 3670016 | tf_op jit(solution)/shard_map/attend/pallas_call | solution.py:214
  78.2 35.3 %all-to-all-done.in_ref = bf16[16,4,2,64,128]{4,3,2,1,0:T(8,128)(2,1)} async-done(((bf16[16,4,2,64,128]{4,3,2,1,0:T(8,128)(2,1)}), bf16[16,4,2,64,128]{4,3,2,1,0:T(8,128)(2,1)}, u32[]{:S(2)}, u32[]{:S(2)}) %all-to-all-start) | async-done | bytes 2097184 | tf_op jit(solution)/shard_map/all_to_all | solution.py:259
  113.5 6.5 %all-to-all-start.2 = ((bf16[16,3,2,64,128]{4,3,2,1,0:T(8,128)(2,1)}), bf16[16,3,2,64,128]{4,3,2,1,0:T(8,128)(2,1)}, u32[]{:S(2)}, u32[]{:S(2)}) async-start(bf16[16,3,2,64,128]{4,3,2,1,0:T(8,128)(2,1)} %bitcast.3), calls=%async_computation.2 | async-start | bytes 3145728 | tf_op jit(solution)/shard_map/all_to_all | solution.py:259
  120.0 0.0 copy-start.6
  120.0 12.2 %attend.2 = (bf16[8,3,2,64,128]{4,3,2,1,0:T(8,128)(2,1)}, bf16[8,3,2,64,128]{4,3,2,1,0:T(8,128)(2,1)}, f32[2,2,128]{2,1,0:T(2,128)}) custom-call(s32[1]{0:T(128)} %bitcast.index_ref, bf16[16,4,2,64,128]{4,3,2,1,0:T(8,128)(2,1)} %all-to-all-done.in_ref, f32[1,128]{1,0:T(1,128)} %gain_q_ref.3, f32[1,128]{1,0:T(1,128)} %gain_k_ref.3), custom_call_target="tpu_custom_call" | custom-call | flops 2684354560 | bytes 3670016 | tf_op jit(solution)/shard_map/attend/pallas_call | solution.py:214
  132.2 0.1 collective-permute-start
  132.3 0.0 copy-done.6
  132.3 0.7 add_reduce_fusion
  133.0 1.6 collective-permute-start.1
  134.6 2.0 %collective-permute-done.1 = f32[2,128]{1,0:T(2,128)S(1)} collective-permute-done((f32[2,128]{1,0:T(2,128)S(1)}, f32[2,128]{1,0:T(2,128)S(1)}, u32[]{:S(2)}, u32[]{:S(2)}) %collective-permute-start.1) | collective-permute-done | bytes 1056 | tf_op jit(solution)/shard_map/ppermute | solution.py:244
  136.6 1.5 collective-permute-start.2
  138.1 2.1 %collective-permute-done.2 = f32[2,128]{1,0:T(2,128)S(1)} collective-permute-done((f32[2,128]{1,0:T(2,128)S(1)}, f32[2,128]{1,0:T(2,128)S(1)}, u32[]{:S(2)}, u32[]{:S(2)}) %collective-permute-start.2) | collective-permute-done | bytes 1056 | tf_op jit(solution)/shard_map/ppermute | solution.py:244
  140.2 3.0 %collective-permute-start.3 = (f32[2,128]{1,0:T(2,128)S(1)}, f32[2,128]{1,0:T(2,128)S(1)}, u32[]{:S(2)}, u32[]{:S(2)}) collective-permute-start(f32[2,128]{1,0:T(2,128)S(1)} %add.17), channel_id=1, source_target_pairs={{0,2},{1,3},{2,0},{3,1},{4,6},{5,7},{6,4},{7,5},{8,10},{9,11},{10,... | collective-permute-start | bytes 3080 | tf_op jit(solution)/shard_map/ppermute | solution.py:244
  143.2 2.0 %collective-permute-done.3 = f32[2,128]{1,0:T(2,128)S(1)} collective-permute-done((f32[2,128]{1,0:T(2,128)S(1)}, f32[2,128]{1,0:T(2,128)S(1)}, u32[]{:S(2)}, u32[]{:S(2)}) %collective-permute-start.3) | collective-permute-done | bytes 1056 | tf_op jit(solution)/shard_map/ppermute | solution.py:244
  145.3 3.2 %collective-permute-start.4 = (f32[2,128]{1,0:T(2,128)S(1)}, f32[2,128]{1,0:T(2,128)S(1)}, u32[]{:S(2)}, u32[]{:S(2)}) collective-permute-start(f32[2,128]{1,0:T(2,128)S(1)} %add.18), channel_id=1, source_target_pairs={{0,4},{1,5},{2,6},{3,7},{4,0},{5,1},{6,2},{7,3},{8,12},{9,13},{10,... | collective-permute-start | bytes 3080 | tf_op jit(solution)/shard_map/ppermute | solution.py:244
  148.5 1.9 collective-permute-done.4
  150.4 0.6 add.19
  150.9 0.0 collective-permute-done.other_ref
  150.9 0.0 copy-start
  150.9 0.9 copy-done
  151.8 2.3 %compose.1 = (bf16[2,3,2,64,128]{4,3,2,1,0:T(8,128)(2,1)}, bf16[2,3,2,64,128]{4,3,2,1,0:T(8,128)(2,1)}, bf16[2,3,2,64,128]{4,3,2,1,0:T(8,128)(2,1)}, bf16[2,3,2,...) custom-call(s32[1]{0:T(128)} %bitcast.index_ref, ...), custom_call_target="tpu_custom_call" | custom-call | tf_op jit(solution)/shard_map/compose/pallas_call | solution.py:65
  154.1 0.4 collective-permute-start.8
  154.5 1.7 collective-permute-start.5
  156.2 3.9 %collective-permute-start.11 = (bf16[2,3,2,64,128]{4,3,2,1,0:T(8,128)(2,1)}, bf16[2,3,2,64,128]{4,3,2,1,0:T(8,128)(2,1)S(1)}, u32[]{:S(2)}, u32[]{:S(2)}) collective-permute-start(bf16[2,3,2,64,128]{4,3,2,1,0:T(8,128)(2,1)} %get-tuple-element.48), channel_id=1, source_target_pairs={{0,96},{8,40},{16,112},{24,56},{32,0},{40,72},{48,16},{56,88},{64,... | collective-permute-start | bytes 589832 | tf_op jit(solution)/shard_map/ppermute | solution.py:267
  160.1 1.2 collective-permute-start.7
  161.2 2.4 %collective-permute-start.6 = (bf16[2,3,2,64,128]{4,3,2,1,0:T(8,128)(2,1)}, bf16[2,3,2,64,128]{4,3,2,1,0:T(8,128)(2,1)S(1)}, u32[]{:S(2)}, u32[]{:S(2)}) collective-permute-start(bf16[2,3,2,64,128]{4,3,2,1,0:T(8,128)(2,1)} %get-tuple-element.38), channel_id=1, source_target_pairs={{0,32},{8,104},{16,48},{24,120},{32,64},{40,8},{48,80},{56,24},{64... | collective-permute-start | bytes 589832 | tf_op jit(solution)/shard_map/ppermute | solution.py:267
  163.6 0.0 collective-permute-done.8.refs_7_
  163.6 0.0 copy-start.1
  163.6 5.1 %collective-permute-start.9 = (bf16[2,3,2,64,128]{4,3,2,1,0:T(8,128)(2,1)}, bf16[2,3,2,64,128]{4,3,2,1,0:T(8,128)(2,1)}, u32[]{:S(2)}, u32[]{:S(2)}) collective-permute-start(bf16[2,3,2,64,128]{4,3,2,1,0:T(8,128)(2,1)} %get-tuple-element.44), channel_id=1, source_target_pairs={{0,64},{8,72},{16,80},{24,88},{32,96},{40,104},{48,112},{56,120},{... | collective-permute-start | bytes 589832 | tf_op jit(solution)/shard_map/ppermute | solution.py:267
  168.7 0.0 collective-permute-done.5.refs_1_
  168.7 0.0 copy-start.2
  168.7 0.1 collective-permute-start.10
  168.8 0.0 all-to-all-done.2.in_ref
  168.8 2.4 %unpack_whole.1 = (bf16[2,2,64,2048]{3,2,1,0:T(8,128)(2,1)}, bf16[2,2,64,2048]{3,2,1,0:T(8,128)(2,1)}, bf16[2,2,64,2048]{3,2,1,0:T(8,128)(2,1)}) custom-call(bf16[16,3,2,64,128]{4,3,2,1,0:T(8,128)(2,1)} %all-to-all-done.2.in_ref), custom_call_target="tpu_custom_call" | custom-call | tf_op jit(solution)/shard_map/unpack_whole/pallas_call | solution.py:89
  171.3 0.9 collective-permute-done.11.refs_6_
  172.2 0.0 copy-start.3
  172.2 8.2 %collective-permute-done.7.refs_3_ = bf16[2,3,2,64,128]{4,3,2,1,0:T(8,128)(2,1)S(1)} collective-permute-done((bf16[2,3,2,64,128]{4,3,2,1,0:T(8,128)(2,1)}, bf16[2,3,2,64,128]{4,3,2,1,0:T(8,128)(2,1)S(1)}, u32[]{:S(2)}, u32[]{:S(2)}) %collective-permute-start.7) | collective-permute-done | bytes 196640 | tf_op jit(solution)/shard_map/ppermute | solution.py:267
  180.4 0.0 copy-start.4
  180.4 9.0 %collective-permute-done.6.refs_2_ = bf16[2,3,2,64,128]{4,3,2,1,0:T(8,128)(2,1)S(1)} collective-permute-done((bf16[2,3,2,64,128]{4,3,2,1,0:T(8,128)(2,1)}, bf16[2,3,2,64,128]{4,3,2,1,0:T(8,128)(2,1)S(1)}, u32[]{:S(2)}, u32[]{:S(2)}) %collective-permute-start.6) | collective-permute-done | bytes 196640 | tf_op jit(solution)/shard_map/ppermute | solution.py:267
  189.4 0.0 copy-start.5
  189.4 0.0 collective-permute-done.9.refs_4_
  189.4 1.9 collective-permute-done.10.refs_5_
  191.3 0.0 copy-done.1
  191.3 0.0 copy-done.2
  191.3 0.0 copy-done.3
  191.3 0.0 copy-done.4
  191.3 0.0 copy-done.5
  191.3 2.6 %unpack.1 = (bf16[2,2,64,2048]{3,2,1,0:T(8,128)(2,1)}, bf16[2,2,64,2048]{3,2,1,0:T(8,128)(2,1)}, bf16[2,2,64,2048]{3,2,1,0:T(8,128)(2,1)}) custom-call(s32[1]{0:T(128)} %bitcast.index_ref, bf16[2,3,2,64,128]{4,3,2,1,0:T(8,128)(2,1)} %get-tuple-element.32.refs_0_, ...), custom_call_target="tpu_custom_call", output_to_operand_aliasing={{0}: (9, {}), {1}: (10, {}), {2}: (11, {})} | custom-call | tf_op jit(solution)/shard_map/unpack/pallas_call | solution.py:114
  (3 shorter events, 0.0 us)
Async XLA Ops:
  3.4 56.1 %all-to-all-start.1 = ((bf16[16,4,2,64,128]{4,3,2,1,0:T(8,128)(2,1)}), bf16[16,4,2,64,128]{4,3,2,1,0:T(8,128)(2,1)}, u32[]{:S(2)}, u32[]{:S(2)}) async-start(bf16[16,4,2,64,128]{4,3,2,1,0:T(8,128)(2,1)} %pack.3), calls=%async_computation.1 | async-start | bytes 4194304 | tf_op jit(solution)/shard_map/all_to_all | solution.py:259
  59.4 54.0 %all-to-all-start = ((bf16[16,4,2,64,128]{4,3,2,1,0:T(8,128)(2,1)}), bf16[16,4,2,64,128]{4,3,2,1,0:T(8,128)(2,1)}, u32[]{:S(2)}, u32[]{:S(2)}) async-start(bf16[16,4,2,64,128]{4,3,2,1,0:T(8,128)(2,1)} %pack.2), calls=%async_computation | async-start | bytes 4194304 | tf_op jit(solution)/shard_map/all_to_all | solution.py:259
  113.5 55.4 %all-to-all-start.2 = ((bf16[16,3,2,64,128]{4,3,2,1,0:T(8,128)(2,1)}), bf16[16,3,2,64,128]{4,3,2,1,0:T(8,128)(2,1)}, u32[]{:S(2)}, u32[]{:S(2)}) async-start(bf16[16,3,2,64,128]{4,3,2,1,0:T(8,128)(2,1)} %bitcast.3), calls=%async_computation.2 | async-start | bytes 3145728 | tf_op jit(solution)/shard_map/all_to_all | solution.py:259
  120.0 12.3 %copy-start.6 = (f32[2,2,128]{2,1,0:T(2,128)S(1)}, f32[2,2,128]{2,1,0:T(2,128)}, u32[]{:S(2)}) copy-start(f32[2,2,128]{2,1,0:T(2,128)} %get-tuple-element.34) | copy-start | bytes 6148
  132.2 18.7 %collective-permute-start = (bf16[8,3,2,64,128]{4,3,2,1,0:T(8,128)(2,1)}, bf16[8,3,2,64,128]{4,3,2,1,0:T(8,128)(2,1)S(1)}, u32[]{:S(2)}, u32[]{:S(2)}) collective-permute-start(bf16[8,3,2,64,128]{4,3,2,1,0:T(8,128)(2,1)} %get-tuple-element.31), channel_id=1, source_target_pairs={{0,8},{8,0},{16,24},{24,16},{32,40},{40,32},{48,56},{56,48},{64,72... | collective-permute-start | bytes 2359304 | tf_op jit(solution)/shard_map/ppermute | solution.py:255
  133.0 3.6 %collective-permute-start.1 = (f32[2,128]{1,0:T(2,128)S(1)}, f32[2,128]{1,0:T(2,128)S(1)}, u32[]{:S(2)}, u32[]{:S(2)}) collective-permute-start(f32[2,128]{1,0:T(2,128)S(1)} %add_reduce_fusion), channel_id=1, source_target_pairs={{0,128},{128,0},{1,129},{129,1},{2,130},{130,2},{3,131},{131,3},{4... | collective-permute-start | bytes 3080 | tf_op jit(solution)/shard_map/ppermute | solution.py:244
  136.6 3.6 %collective-permute-start.2 = (f32[2,128]{1,0:T(2,128)S(1)}, f32[2,128]{1,0:T(2,128)S(1)}, u32[]{:S(2)}, u32[]{:S(2)}) collective-permute-start(f32[2,128]{1,0:T(2,128)S(1)} %add.16), channel_id=1, source_target_pairs={{0,1},{1,0},{2,3},{3,2},{4,5},{5,4},{6,7},{7,6},{8,9},{9,8},{10,11... | collective-permute-start | bytes 3080 | tf_op jit(solution)/shard_map/ppermute | solution.py:244
  140.2 5.1 %collective-permute-start.3 = (f32[2,128]{1,0:T(2,128)S(1)}, f32[2,128]{1,0:T(2,128)S(1)}, u32[]{:S(2)}, u32[]{:S(2)}) collective-permute-start(f32[2,128]{1,0:T(2,128)S(1)} %add.17), channel_id=1, source_target_pairs={{0,2},{1,3},{2,0},{3,1},{4,6},{5,7},{6,4},{7,5},{8,10},{9,11},{10,... | collective-permute-start | bytes 3080 | tf_op jit(solution)/shard_map/ppermute | solution.py:244
  145.3 5.1 %collective-permute-start.4 = (f32[2,128]{1,0:T(2,128)S(1)}, f32[2,128]{1,0:T(2,128)S(1)}, u32[]{:S(2)}, u32[]{:S(2)}) collective-permute-start(f32[2,128]{1,0:T(2,128)S(1)} %add.18), channel_id=1, source_target_pairs={{0,4},{1,5},{2,6},{3,7},{4,0},{5,1},{6,2},{7,3},{8,12},{9,13},{10,... | collective-permute-start | bytes 3080 | tf_op jit(solution)/shard_map/ppermute | solution.py:244
  150.9 0.9 copy-start
  154.1 9.5 %collective-permute-start.8 = (bf16[2,3,2,64,128]{4,3,2,1,0:T(8,128)(2,1)}, bf16[2,3,2,64,128]{4,3,2,1,0:T(8,128)(2,1)S(1)}, u32[]{:S(2)}, u32[]{:S(2)}) collective-permute-start(bf16[2,3,2,64,128]{4,3,2,1,0:T(8,128)(2,1)} %get-tuple-element.43), channel_id=1, source_target_pairs={{0,112},{8,24},{16,0},{24,40},{32,16},{40,56},{48,32},{56,72},{64,... | collective-permute-start | bytes 589832 | tf_op jit(solution)/shard_map/ppermute | solution.py:267
  154.5 14.2 %collective-permute-start.5 = (bf16[2,3,2,64,128]{4,3,2,1,0:T(8,128)(2,1)}, bf16[2,3,2,64,128]{4,3,2,1,0:T(8,128)(2,1)S(1)}, u32[]{:S(2)}, u32[]{:S(2)}) collective-permute-start(bf16[2,3,2,64,128]{4,3,2,1,0:T(8,128)(2,1)} %get-tuple-element.36), channel_id=1, source_target_pairs={{0,16},{8,120},{16,32},{24,8},{32,48},{40,24},{48,64},{56,40},{64,... | collective-permute-start | bytes 589832 | tf_op jit(solution)/shard_map/ppermute | solution.py:267
  156.2 16.0 %collective-permute-start.11 = (bf16[2,3,2,64,128]{4,3,2,1,0:T(8,128)(2,1)}, bf16[2,3,2,64,128]{4,3,2,1,0:T(8,128)(2,1)S(1)}, u32[]{:S(2)}, u32[]{:S(2)}) collective-permute-start(bf16[2,3,2,64,128]{4,3,2,1,0:T(8,128)(2,1)} %get-tuple-element.48), channel_id=1, source_target_pairs={{0,96},{8,40},{16,112},{24,56},{32,0},{40,72},{48,16},{56,88},{64,... | collective-permute-start | bytes 589832 | tf_op jit(solution)/shard_map/ppermute | solution.py:267
  160.1 20.3 %collective-permute-start.7 = (bf16[2,3,2,64,128]{4,3,2,1,0:T(8,128)(2,1)}, bf16[2,3,2,64,128]{4,3,2,1,0:T(8,128)(2,1)S(1)}, u32[]{:S(2)}, u32[]{:S(2)}) collective-permute-start(bf16[2,3,2,64,128]{4,3,2,1,0:T(8,128)(2,1)} %get-tuple-element.40), channel_id=1, source_target_pairs={{0,48},{8,88},{16,64},{24,104},{32,80},{40,120},{48,96},{56,8},{64... | collective-permute-start | bytes 589832 | tf_op jit(solution)/shard_map/ppermute | solution.py:267
  161.2 28.1 %collective-permute-start.6 = (bf16[2,3,2,64,128]{4,3,2,1,0:T(8,128)(2,1)}, bf16[2,3,2,64,128]{4,3,2,1,0:T(8,128)(2,1)S(1)}, u32[]{:S(2)}, u32[]{:S(2)}) collective-permute-start(bf16[2,3,2,64,128]{4,3,2,1,0:T(8,128)(2,1)} %get-tuple-element.38), channel_id=1, source_target_pairs={{0,32},{8,104},{16,48},{24,120},{32,64},{40,8},{48,80},{56,24},{64... | collective-permute-start | bytes 589832 | tf_op jit(solution)/shard_map/ppermute | solution.py:267
  163.6 27.7 %copy-start.1 = (bf16[2,3,2,64,128]{4,3,2,1,0:T(8,128)(2,1)}, bf16[2,3,2,64,128]{4,3,2,1,0:T(8,128)(2,1)S(1)}, u32[]{:S(2)}) copy-start(bf16[2,3,2,64,128]{4,3,2,1,0:T(8,128)(2,1)S(1)} %collective-permute-done.8.refs_7_) | copy-start | bytes 589828
  163.6 25.8 %collective-permute-start.9 = (bf16[2,3,2,64,128]{4,3,2,1,0:T(8,128)(2,1)}, bf16[2,3,2,64,128]{4,3,2,1,0:T(8,128)(2,1)}, u32[]{:S(2)}, u32[]{:S(2)}) collective-permute-start(bf16[2,3,2,64,128]{4,3,2,1,0:T(8,128)(2,1)} %get-tuple-element.44), channel_id=1, source_target_pairs={{0,64},{8,72},{16,80},{24,88},{32,96},{40,104},{48,112},{56,120},{... | collective-permute-start | bytes 589832 | tf_op jit(solution)/shard_map/ppermute | solution.py:267
  168.7 22.6 %copy-start.2 = (bf16[2,3,2,64,128]{4,3,2,1,0:T(8,128)(2,1)}, bf16[2,3,2,64,128]{4,3,2,1,0:T(8,128)(2,1)S(1)}, u32[]{:S(2)}) copy-start(bf16[2,3,2,64,128]{4,3,2,1,0:T(8,128)(2,1)S(1)} %collective-permute-done.5.refs_1_) | copy-start | bytes 589828
  168.7 22.6 %collective-permute-start.10 = (bf16[2,3,2,64,128]{4,3,2,1,0:T(8,128)(2,1)}, bf16[2,3,2,64,128]{4,3,2,1,0:T(8,128)(2,1)}, u32[]{:S(2)}, u32[]{:S(2)}) collective-permute-start(bf16[2,3,2,64,128]{4,3,2,1,0:T(8,128)(2,1)} %get-tuple-element.46), channel_id=1, source_target_pairs={{0,80},{8,56},{16,96},{24,72},{32,112},{40,88},{48,0},{56,104},{64... | collective-permute-start | bytes 589832 | tf_op jit(solution)/shard_map/ppermute | solution.py:267
  172.2 19.1 %copy-start.3 = (bf16[2,3,2,64,128]{4,3,2,1,0:T(8,128)(2,1)}, bf16[2,3,2,64,128]{4,3,2,1,0:T(8,128)(2,1)S(1)}, u32[]{:S(2)}) copy-start(bf16[2,3,2,64,128]{4,3,2,1,0:T(8,128)(2,1)S(1)} %collective-permute-done.11.refs_6_) | copy-start | bytes 589828
  180.4 11.0 %copy-start.4 = (bf16[2,3,2,64,128]{4,3,2,1,0:T(8,128)(2,1)}, bf16[2,3,2,64,128]{4,3,2,1,0:T(8,128)(2,1)S(1)}, u32[]{:S(2)}) copy-start(bf16[2,3,2,64,128]{4,3,2,1,0:T(8,128)(2,1)S(1)} %collective-permute-done.7.refs_3_) | copy-start | bytes 589828
  189.4 2.0 %copy-start.5 = (bf16[2,3,2,64,128]{4,3,2,1,0:T(8,128)(2,1)}, bf16[2,3,2,64,128]{4,3,2,1,0:T(8,128)(2,1)S(1)}, u32[]{:S(2)}) copy-start(bf16[2,3,2,64,128]{4,3,2,1,0:T(8,128)(2,1)S(1)} %collective-permute-done.6.refs_2_) | copy-start | bytes 589828
